TPU v7x, 32 devices: a whole 2x2x4 slice. The times are simulated.
32 devices in a mesh: dp: 4 (over x, core), fsdp: 8 (over z, y).
Axes of the slice: x: 2, y: 2, z: 4, core: 2. Of those that a mesh axis runs over, the one named last changes fastest.
Arguments:
- xbc: bfloat16 [4096, 10240], P(('dp', 'fsdp')), may hold values from -6 to 6
- zgate: bfloat16 [4096, 8192], P(('dp', 'fsdp')), may hold values from -6 to 6
- dt_raw: float32 [4096, 128], P(('dp', 'fsdp')), may hold values from -5 to 5
- prompt_states: bfloat16 [8, 128, 64, 128], P(None, ('dp', 'fsdp')), may hold values from -3 to 3
- conv_tails: bfloat16 [8, 3, 10240], P(None, None, ('dp', 'fsdp')), may hold values from -6 to 6
- resp_prompt: int32 [128], replicated, may hold values from 0 to 7, as said below
- resp_lengths: int32 [32, 4], P(('dp', 'fsdp')), may hold values from 1 to 80, 128 in all within a row
- rewards: float32 [128], replicated, may hold values from -4 to 4
- upstream: bfloat16 [4096, 8192], P(('dp', 'fsdp')), may hold values from -6 to 6
- conv_weight: float32 [4, 10240], P(None, 'fsdp'), may hold values from -3 to 3
- conv_bias: float32 [10240], P('fsdp'), may hold values from -3 to 3
- dt_bias: float32 [128], P('fsdp'), may hold values from -3 to -1
- a_log: float32 [128], P('fsdp'), may hold values from -5 to -0.7
- d_skip: float32 [128], P('fsdp'), may hold values from 0.5 to 1.5
- norm_gain: float32 [8192], P('fsdp'), may hold values from 0.5 to 1.5
Outputs:
- grad_xbc: bfloat16 [4096, 10240], P(('dp', 'fsdp'))
- grad_zgate: bfloat16 [4096, 8192], P(('dp', 'fsdp'))
- grad_dt_raw: float32 [4096, 128], P(('dp', 'fsdp'))
- grad_prompt_states: float32 [8, 128, 64, 128], P(None, ('dp', 'fsdp'))
- grad_conv_tails: float32 [8, 3, 10240], P(None, None, ('dp', 'fsdp'))
- grad_conv_weight: float32 [4, 10240], P(None, 'fsdp')
- grad_conv_bias: float32 [10240], P('fsdp')
- grad_dt_bias: float32 [128], P('fsdp')
- grad_a_log: float32 [128], P('fsdp')
- grad_d_skip: float32 [128], P('fsdp')
- grad_norm_gain: float32 [8192], P('fsdp')
Inputs may be any that keep to these rules, and one draw needn't show every extreme that they name: `resp_prompt`: each of the 8 prompts is named by exactly 16 responses. `resp_lengths`: the 4 lengths of one device sum to 128.
All inputs are finite; a program needn't handle non-finite values.
Results may differ from a plain program's by a relative error of at most 0.0011.
Values may be sent and summed in bfloat16 or wider, within the bound.
A program may use at most 192 MiB of HBM per device.

v0:
```python
import jax
import jax.numpy as jnp
from jax import lax
from jax.sharding import PartitionSpec as P

GROUP = 16
H = 128
P_SIZE = 64
N = 128
G = 8
GS = 2048


def advantages(rewards, resp_prompt, prompt_count):
    member = (resp_prompt[:, None] == jnp.arange(prompt_count, dtype=jnp.int32)[None, :]).astype(
        jnp.float32
    )
    group_mean = jnp.dot(rewards, member, precision=lax.Precision.HIGHEST) / GROUP
    centred = rewards - jnp.dot(member, group_mean, precision=lax.Precision.HIGHEST)
    spread = jnp.sqrt(jnp.dot(centred * centred, member, precision=lax.Precision.HIGHEST) / GROUP)
    return centred / jnp.dot(member, jnp.maximum(spread, 0.8), precision=lax.Precision.HIGHEST)


def token_layout(lengths, row_count):
    places = jnp.arange(row_count, dtype=jnp.int32)
    doc_ends = jnp.cumsum(lengths)
    doc_starts = doc_ends - lengths
    member = (places[:, None] >= doc_starts[None, :]) & (places[:, None] < doc_ends[None, :])
    start_tok = jnp.sum(jnp.where(member, doc_starts[None, :], 0), axis=1)
    return (member, start_tok, places - start_tok)


def conv_branch(signal, tail_rows, conv_w, conv_b, member, offset):
    row_count = signal.shape[0]
    summed = conv_w[3][None, :] * signal
    for delay_step in (1, 2, 3):
        lagged = jnp.concatenate(
            [jnp.zeros((delay_step, signal.shape[1]), jnp.float32), signal[:-delay_step]], axis=0
        )
        summed = (
            summed
            + jnp.where((offset >= delay_step)[:, None], lagged, 0.0)
            * conv_w[3 - delay_step][None, :]
        )
    tail_a = tail_rows[:, 0, :]
    tail_b = tail_rows[:, 1, :]
    tail_c = tail_rows[:, 2, :]
    w_zero = conv_w[0][None, :]
    w_one = conv_w[1][None, :]
    w_two = conv_w[2][None, :]
    lead_in = jnp.stack(
        [
            w_two * tail_c + w_one * tail_b + w_zero * tail_a,
            w_one * tail_c + w_zero * tail_b,
            w_zero * tail_c,
        ],
        axis=1,
    )
    select = (
        member[:, :, None]
        & (offset[:, None, None] == jnp.arange(3, dtype=jnp.int32)[None, None, :])
    ).astype(jnp.float32)
    summed = summed + jnp.dot(
        select.reshape(row_count, -1),
        lead_in.reshape(-1, signal.shape[1]),
        precision=lax.Precision.HIGHEST,
    )
    return jax.nn.silu(summed + conv_b[None, :])


def mixer_forward(signal, gate_in, dt_in, states, tail_rows, params, member, start_tok, offset):
    conv_w, conv_b, bias_dt, log_rate, skip_all, gain = params
    row_count = signal.shape[0]
    doc_count = states.shape[0]
    inner = H * P_SIZE
    per_group = H // G
    conv_out = conv_branch(signal, tail_rows, conv_w, conv_b, member, offset)
    x_heads = conv_out[:, :inner].reshape(row_count, G, per_group, P_SIZE).transpose(1, 0, 2, 3)
    b_all = conv_out[:, inner : inner + G * N].reshape(row_count, G, N).transpose(1, 0, 2)
    c_all = conv_out[:, inner + G * N :].reshape(row_count, G, N).transpose(1, 0, 2)
    step_size = jax.nn.softplus(dt_in + bias_dt[None, :])
    decay_log = -step_size * jnp.exp(log_rate)[None, :]
    cum_log = jnp.cumsum(decay_log, axis=0)
    base_log = jnp.take(cum_log - decay_log, start_tok, axis=0)
    rel_log = cum_log - base_log
    places = jnp.arange(row_count, dtype=jnp.int32)
    causal = (start_tok[:, None] == start_tok[None, :]) & (places[:, None] >= places[None, :])
    member_f = member.astype(jnp.float32)

    def by_group(table):
        return table.reshape(row_count, G, per_group).transpose(1, 0, 2)

    start_all = states.reshape(doc_count, G, per_group, P_SIZE, N).transpose(1, 0, 2, 3, 4)

    def group_mix(items):
        c_rows, b_rows, x_rows, steps_g, cum_g, rel_g, start_state, skip_gain = items
        scores = jnp.dot(c_rows, b_rows.T, precision=lax.Precision.HIGHEST)
        log_gaps = cum_g.T[:, :, None] - cum_g.T[:, None, :]
        decays = jnp.exp(jnp.where(causal[None], log_gaps, -jnp.inf))
        weights = decays * scores[None] * steps_g.T[:, None, :]
        within = jnp.einsum("kts,skp->tkp", weights, x_rows, precision=lax.Precision.HIGHEST)
        c_masked = member_f[:, :, None] * c_rows[:, None, :]
        carried = jnp.einsum(
            "tdn,dkpn->tkp", c_masked, start_state, precision=lax.Precision.HIGHEST
        )
        carried = carried * jnp.exp(rel_g)[:, :, None]
        return within + carried + skip_gain[None, :, None] * x_rows

    mixed_out = lax.map(
        jax.checkpoint(group_mix),
        (
            c_all,
            b_all,
            x_heads,
            by_group(step_size),
            by_group(cum_log),
            by_group(rel_log),
            start_all,
            skip_all.reshape(G, per_group),
        ),
    )
    mixed_out = mixed_out.transpose(1, 0, 2, 3).reshape(row_count, inner)
    gated_out = mixed_out * jax.nn.silu(gate_in)
    grouped = gated_out.reshape(row_count, inner // GS, GS)
    inv_rms = lax.rsqrt(jnp.mean(grouped * grouped, axis=-1, keepdims=True) + 1e-05)
    return (grouped * inv_rms).reshape(row_count, inner) * gain[None, :]


def local_grads(
    signal_in, gate_in, dt_in, states, tail_rows, params, lengths, upstream, doc_weight
):
    member, start_tok, offset = token_layout(lengths, signal_in.shape[0])
    tok_weight = jnp.sum(jnp.where(member, doc_weight[None, :], 0.0), axis=1)

    def forward(signal, gate_vals, dt_vals, state_vals, tail_vals, weight_vals):
        return mixer_forward(
            signal,
            gate_vals,
            dt_vals,
            state_vals,
            tail_vals,
            weight_vals,
            member,
            start_tok,
            offset,
        )

    primal_out, pullback = jax.vjp(
        forward,
        signal_in.astype(jnp.float32),
        gate_in.astype(jnp.float32),
        dt_in,
        states.astype(jnp.float32),
        tail_rows.astype(jnp.float32),
        params,
    )
    return pullback(upstream.astype(jnp.float32) * tok_weight[:, None])


def shards(
    xbc,
    zgate,
    dt_raw,
    prompt_states,
    conv_tails,
    resp_prompt,
    resp_lengths,
    rewards,
    upstream,
    conv_weight,
    conv_bias,
    dt_bias,
    a_log,
    d_skip,
    norm_gain,
):
    dp_count = lax.axis_size("dp")
    fsdp_count = lax.axis_size("fsdp")
    holders = dp_count * fsdp_count
    holder = lax.axis_index(("dp", "fsdp"))
    params = (
        lax.all_gather(conv_weight, "fsdp", axis=1, tiled=True),
        lax.all_gather(conv_bias, "fsdp", axis=0, tiled=True),
        lax.all_gather(dt_bias, "fsdp", axis=0, tiled=True),
        lax.all_gather(a_log, "fsdp", axis=0, tiled=True),
        lax.all_gather(d_skip, "fsdp", axis=0, tiled=True),
        lax.all_gather(norm_gain, "fsdp", axis=0, tiled=True),
    )
    doc_count = resp_lengths.shape[1]
    lengths = resp_lengths[0]
    prompt_count = prompt_states.shape[0]
    head_share = prompt_states.shape[1]
    chan_share = conv_tails.shape[2]
    responses = holders * doc_count
    state_rows = prompt_states[resp_prompt]
    tail_sent = conv_tails[resp_prompt]
    got_states, got_tails = (
        lax.all_to_all(
            state_rows.reshape(holders, doc_count, 1, head_share, P_SIZE, N),
            ("dp", "fsdp"),
            split_axis=0,
            concat_axis=2,
            tiled=True,
        ),
        lax.all_to_all(
            tail_sent.reshape(holders, doc_count, 1, 3, chan_share),
            ("dp", "fsdp"),
            split_axis=0,
            concat_axis=2,
            tiled=True,
        ),
    )
    states = got_states.reshape(doc_count, holders * head_share, P_SIZE, N)
    tail_rows = (
        got_tails.reshape(doc_count, holders, 3, chan_share)
        .transpose(0, 2, 1, 3)
        .reshape(doc_count, 3, holders * chan_share)
    )
    advantage = advantages(rewards, resp_prompt, prompt_count)
    row_count = xbc.shape[0]
    doc_weight = lax.dynamic_slice_in_dim(advantage, holder * doc_count, doc_count) * (
        row_count / (doc_count * lengths.astype(jnp.float32))
    )
    gradients = local_grads(
        xbc, zgate, dt_raw, states, tail_rows, params, lengths, upstream, doc_weight
    )
    grad_x, grad_z, grad_dt, grad_state, grad_tail, grad_param = gradients
    tail_back = grad_tail.reshape(doc_count, 3, holders, chan_share).transpose(0, 2, 1, 3)
    back_state, back_tail = (
        lax.all_to_all(
            grad_state.reshape(1, doc_count, holders, head_share, P_SIZE, N),
            ("dp", "fsdp"),
            split_axis=2,
            concat_axis=0,
            tiled=True,
        ),
        lax.all_to_all(
            tail_back.reshape(1, doc_count, holders, 3, chan_share),
            ("dp", "fsdp"),
            split_axis=2,
            concat_axis=0,
            tiled=True,
        ),
    )
    prompt_onehot = (
        jnp.arange(prompt_count, dtype=jnp.int32)[:, None] == resp_prompt[None, :]
    ).astype(jnp.float32)
    grad_states_out = jnp.dot(
        prompt_onehot,
        back_state.reshape(responses, head_share * P_SIZE * N),
        precision=lax.Precision.HIGHEST,
    ).reshape(prompt_count, head_share, P_SIZE, N)
    grad_tails_out = jnp.dot(
        prompt_onehot, back_tail.reshape(responses, 3 * chan_share), precision=lax.Precision.HIGHEST
    ).reshape(prompt_count, 3, chan_share)
    shares = (
        lax.psum_scatter(grad_param[0], "fsdp", scatter_dimension=1, tiled=True),
        lax.psum_scatter(grad_param[1], "fsdp", scatter_dimension=0, tiled=True),
        lax.psum_scatter(grad_param[2], "fsdp", scatter_dimension=0, tiled=True),
        lax.psum_scatter(grad_param[3], "fsdp", scatter_dimension=0, tiled=True),
        lax.psum_scatter(grad_param[4], "fsdp", scatter_dimension=0, tiled=True),
        lax.psum_scatter(grad_param[5], "fsdp", scatter_dimension=0, tiled=True),
    )
    totals = lax.psum(shares, "dp")
    return (
        grad_x.astype(jnp.bfloat16),
        grad_z.astype(jnp.bfloat16),
        grad_dt,
        grad_states_out,
        grad_tails_out,
        totals[0],
        totals[1],
        totals[2],
        totals[3],
        totals[4],
        totals[5],
    )


def solution(mesh):
    return jax.shard_map(
        shards,
        mesh=mesh,
        in_specs=(
            P(("dp", "fsdp"), None),
            P(("dp", "fsdp"), None),
            P(("dp", "fsdp"), None),
            P(None, ("dp", "fsdp"), None, None),
            P(None, None, ("dp", "fsdp")),
            P(),
            P(("dp", "fsdp"), None),
            P(),
            P(("dp", "fsdp"), None),
            P(None, "fsdp"),
            P("fsdp"),
            P("fsdp"),
            P("fsdp"),
            P("fsdp"),
            P("fsdp"),
        ),
        out_specs=(
            P(("dp", "fsdp"), None),
            P(("dp", "fsdp"), None),
            P(("dp", "fsdp"), None),
            P(None, ("dp", "fsdp"), None, None),
            P(None, None, ("dp", "fsdp")),
            P(None, "fsdp"),
            P("fsdp"),
            P("fsdp"),
            P("fsdp"),
            P("fsdp"),
            P("fsdp"),
        ),
        check_vma=False,
    )
```

profile of v0, /device:TPU:0, one launch (start us, length us, event | category | flops | bytes accessed | tf_op | source)
XLA Modules:
  0.0 1241.1 jit_solution(11263181394660054232)
XLA Ops:
  11.2 7.3 all-to-all-start
  18.5 6.5 gather_fusion.2
  25.0 9.6 copy.110
  34.6 6.0 all-to-all-start.1
  51.3 148.0 %all-reduce.28 = (f32[128]{0:T(128)S(1)}, f32[128]{0:T(128)S(1)}, f32[128]{0:T(128)S(1)}) all-reduce(f32[128]{0:T(128)S(1)} %dynamic-update-slice, f32[128]{0:T(128)S(1)} %dynamic-update-slice.1, f32[128]{0:T(128)S(1)} %dynamic-update-slice.2), channel_id=1, replica_groups=mesh['dp'=4,'fsdp'=8] {'fsdp'}, use_global_device_ids=true, to_apply=%add.19 | all-reduce | flops 384 | bytes 3072
  214.0 64.8 %all_gather.23 = f32[8192]{0:T(1024)} all-gather(f32[1024]{0:T(1024)S(1)} %copy-done.29), channel_id=1, replica_groups=mesh['dp'=4,'fsdp'=8] {'fsdp'}, dimensions={0}, use_global_device_ids=true | all-gather | bytes 36864 | tf_op jit(solution)/shard_map/all_gather | solution.py:187
  278.8 30.6 %all-gather = f32[8,1,1280]{2,1,0:T(1,128)S(1)} all-gather(f32[1,1,1280]{2,1,0:T(1,128)S(1)} %reshape.671), channel_id=1, replica_groups=mesh['dp'=4,'fsdp'=8] {'fsdp'}, dimensions={0}, use_global_device_ids=true | all-gather | bytes 46080 | tf_op jit(solution)/shard_map/all_gather | solution.py:183
  309.4 30.6 %all_gather.18 = f32[4,10240]{1,0:T(4,128)S(1)} all-gather(f32[4,1280]{1,0:T(4,128)S(1)} %copy-done.22), channel_id=1, replica_groups=mesh['dp'=4,'fsdp'=8] {'fsdp'}, dimensions={1}, use_global_device_ids=true | all-gather | bytes 184320 | tf_op jit(solution)/shard_map/all_gather | solution.py:182
  347.1 13.3 %fusion.99 = (f32[128,10240]{1,0:T(8,128)S(1)}, f32[128,10240]{1,0:T(8,128)}) fusion(f32[10240]{0:T(1024)S(1)} %bitcast.531, f32[4,1,10240]{2,1,0:T(1,128)S(1)} %get-tuple-element.786, f32[4,1,10240]{2,1,0:T(1,128)S(1)} %get-tuple-element.784, f32[4,1,10240]{2,1,0:T(1,128)S(1)} %get-tuple-element.783, pred[128,3]{0,1:T(4,128)(4,1)S(1)} %copy-done.47, ...), kind=kOutput, calls=%fused_computation.150 | convolution fusion | flops 211273216 | bytes 29287680 | tf_op jit(solution)/shard_map/jvp()/dot_general | solution.py:63
  373.1 11.5 bitcast_convert_fusion
  387.1 89.4 %while.41 = (s32[]{:T(128)}, f32[8,128,16,64]{1,3,2,0:T(8,128)}, f32[8,128,16,64]{1,3,2,0:T(8,128)}, f32[8,128,16]{1,2,0:T(8,128)S(1)}, f32[8,128,128]{2,1,0:T(8...) while((s32[]{:T(128)}, f32[8,128,16,64]{1,3,2,0:T(8,128)}, ...), condition=%wide.region_5.6_spmd.clone, body=%wide.region_4.5_spmd.clone.sunk | while | flops 1033439232 | bytes 5282625 | solution.py:109
  482.4 6.7 fusion.105
  493.4 7.9 broadcast_in_dim.266.clone
  501.3 158.2 %while.42 = (s32[]{:T(128)}, f32[8,128,128]{2,1,0:T(8,128)}, f32[8,128,128]{2,1,0:T(8,128)}, f32[8,128,16,64]{1,3,2,0:T(8,128)}, f32[8,128,16]{1,2,0:T(8,128)S(1...) while((s32[]{:T(128)}, f32[8,128,128]{2,1,0:T(8,128)}, ...), condition=%wide.region_16.17_spmd.clone, body=%wide.region_8.16_spmd.clone.sunk | while | flops 2899869696 | bytes 23611008 | solution.py:109
  659.5 5.6 copy.115
  667.4 12.2 fusion.150
  692.6 11.9 copy.120
  704.5 5.8 all-to-all-done.3
  738.2 278.4 %all-reduce.32.cloned.1.call-done = (f32[10240]{0:T(1024)}, f32[128]{0:T(128)}, f32[128]{0:T(128)}, f32[128]{0:T(128)}, f32[8192]{0:T(1024)}) async-done(((f32[10240]{0:T(1024)}, f32[128]{0:T(128)}, f32[128]{0:T(128)}, f32[128]{0:T(128)}, f32[8192]{0:T(1024)}), (f32[10240]{0:T(1024)}, f32[128]{0:T(128)}, f32[128]{0:T(128)}, f32[128]{0:T(128)}, f32[8192]{0:T(1024)})) %all-reduce.32.cloned.1.call-update) | async-done | bytes 75280
  1020.2 150.3 %reduce-scatter.4.cloned.1.call-done = f32[1280,4]{1,0:T(8,128)} async-done(((f32[10240,4]{1,0:T(8,128)}), f32[1280,4]{1,0:T(8,128)}) %reduce-scatter.4.cloned.1.call-update) | async-done | bytes 20496
  1171.9 12.2 all-reduce.29
  1185.9 18.2 %reshape.613 = f32[128,32768]{1,0:T(8,128)} reshape(f32[32,1,4,1,4,64,128]{6,5,4,2,0,3,1:T(8,128)} %bitcast.71) | data formatting | bytes 33554432 | tf_op jit(solution)/shard_map/reshape | solution.py:250
  1204.1 17.4 %copy.121 = f32[32768,128]{1,0:T(8,128)} copy(f32[32768,128]{0,1:T(8,128)} %bitcast.485) | data formatting | bytes 33554432 | tf_op jit(solution)/shard_map/dot_general | solution.py:248
  1221.5 11.2 fusion.136
  (476 shorter events, 356.7 us)
Async XLA Ops:
  11.2 23.5 %all-to-all-start = ((bf16[32,4,1,3,320]{4,1,3,2,0:T(4,128)(2,1)}), bf16[32,4,1,3,320]{4,1,3,2,0:T(4,128)(2,1)S(1)}, u32[]{:S(2)}, u32[]{:S(2)}) async-start(bf16[32,4,1,3,320]{4,1,3,2,0:T(4,128)(2,1)} %copy.99), calls=%async_computation | async-start | bytes 589824 | tf_op jit(solution)/shard_map/all_to_all | solution.py:205
  34.6 338.5 %all-to-all-start.1 = ((bf16[32,4,1,4,64,128]{5,4,1,3,2,0:T(8,128)(2,1)}), bf16[32,4,1,4,64,128]{5,4,1,3,2,0:T(8,128)(2,1)}, u32[]{:S(2)}, u32[]{:S(2)}) async-start(bf16[32,4,1,4,64,128]{5,4,1,3,2,0:T(8,128)(2,1)} %copy.110), calls=%async_computation.1 | async-start | bytes 16777216 | tf_op jit(solution)/shard_map/all_to_all | solution.py:198
  46.3 153.4 %copy-start.14 = (f32[128,128]{1,0:T(8,128)S(1)}, f32[128,128]{1,0:T(8,128)}, u32[]{:S(2)}) copy-start(f32[128,128]{1,0:T(8,128)} %param.21) | copy-start | bytes 196612
  46.3 154.2 %copy-start.45 = (s32[1,4]{1,0:T(1,128)S(1)}, s32[1,4]{1,0:T(1,128)}, u32[]{:S(2)}) copy-start(s32[1,4]{1,0:T(1,128)} %param.25) | copy-start | bytes 52
  46.4 154.4 %copy-start.27 = (f32[1280]{0:T(1024)S(1)}, f32[1280]{0:T(1024)}, u32[]{:S(2)}) copy-start(f32[1280]{0:T(1024)} %param.29) | copy-start | bytes 15364
  46.4 155.1 %copy-start.30 = (s32[128]{0:T(128)S(1)}, s32[128]{0:T(128)}, u32[]{:S(2)}) copy-start(s32[128]{0:T(128)} %param.24) | copy-start | bytes 1540
  46.4 155.1 %copy-start.51 = (f32[128]{0:T(128)S(1)}, f32[128]{0:T(128)}, u32[]{:S(2)}) copy-start(f32[128]{0:T(128)} %param.26) | copy-start | bytes 1540
  49.3 164.7 %copy-start.29 = (f32[1024]{0:T(1024)S(1)}, f32[1024]{0:T(1024)}, u32[]{:S(2)}) copy-start(f32[1024]{0:T(1024)} %param.33) | copy-start | bytes 12292
  49.3 260.1 %copy-start.22 = (f32[4,1280]{1,0:T(4,128)S(1)}, f32[4,1280]{1,0:T(4,128)}, u32[]{:S(2)}) copy-start(f32[4,1280]{1,0:T(4,128)} %param.28) | copy-start | bytes 61444
  202.6 138.1 %copy-start.20 = (s32[4]{0:T(128)}, s32[4]{0:T(128)S(1)}, u32[]{:S(2)}) copy-start(s32[4]{0:T(128)S(1)} %fusion.147) | copy-start | bytes 52
  203.2 137.5 %copy-start.43 = (pred[128,4]{0,1:T(4,128)(4,1)}, pred[128,4]{0,1:T(4,128)(4,1)S(1)}, u32[]{:S(2)}) copy-start(pred[128,4]{0,1:T(4,128)(4,1)S(1)} %get-tuple-element.767) | copy-start | bytes 1540
  214.0 133.1 %copy-start.47 = (pred[128,3]{0,1:T(4,128)(4,1)S(1)}, pred[128,3]{0,1:T(4,128)(4,1)}, u32[]{:S(2)}) copy-start(pred[128,3]{0,1:T(4,128)(4,1)} %copy-done.46) | copy-start | bytes 1156
  340.0 20.5 %copy-start.36 = (pred[128]{0:T(512)(128)(4,1)}, pred[128]{0:T(512)(128)(4,1)S(1)}, u32[]{:S(2)}) copy-start(pred[128]{0:T(512)(128)(4,1)S(1)} %get-tuple-element.804) | copy-start | bytes 388
  340.0 20.5 %copy-start.38 = (pred[128]{0:T(512)(128)(4,1)}, pred[128]{0:T(512)(128)(4,1)S(1)}, u32[]{:S(2)}) copy-start(pred[128]{0:T(512)(128)(4,1)S(1)} %get-tuple-element.806) | copy-start | bytes 388
  340.0 20.5 %copy-start.40 = (pred[128]{0:T(512)(128)(4,1)}, pred[128]{0:T(512)(128)(4,1)S(1)}, u32[]{:S(2)}) copy-start(pred[128]{0:T(512)(128)(4,1)S(1)} %get-tuple-element.805) | copy-start | bytes 388
  341.5 19.0 %copy-start.9 = (f32[1,10240]{1,0:T(1,128)}, f32[1,10240]{1,0:T(1,128)S(1)}, u32[]{:S(2)}) copy-start(f32[1,10240]{1,0:T(1,128)S(1)} %get-tuple-element.793) | copy-start | bytes 122884
  341.5 19.0 %copy-start.11 = (f32[1,10240]{1,0:T(1,128)}, f32[1,10240]{1,0:T(1,128)S(1)}, u32[]{:S(2)}) copy-start(f32[1,10240]{1,0:T(1,128)S(1)} %get-tuple-element.794) | copy-start | bytes 122884
  387.1 89.4 %copy-start.13 = (f32[8192]{0:T(1024)S(1)}, f32[8192]{0:T(1024)}, u32[]{:S(2)}) copy-start(f32[8192]{0:T(1024)} %all_gather.23) | copy-start | bytes 98308
  387.1 89.4 %copy-start.28 = (f32[128]{0:T(128)S(1)}, f32[128]{0:T(128)}, u32[]{:S(2)}) copy-start(f32[128]{0:T(128)} %get-tuple-element.766) | copy-start | bytes 1540
  687.7 22.6 %all-to-all-start.3 = ((f32[1,4,32,3,320]{4,1,3,0,2:T(4,128)}), f32[1,4,32,3,320]{4,1,3,0,2:T(4,128)S(1)}, u32[]{:S(2)}, u32[]{:S(2)}) async-start(f32[1,4,32,3,320]{4,1,3,0,2:T(4,128)} %copy.127), calls=%async_computation.3 | async-start | bytes 1179648 | tf_op jit(solution)/shard_map/all_to_all | solution.py:237
  710.4 475.5 %all-to-all-start.2 = ((f32[1,4,32,4,64,128]{5,4,3,1,0,2:T(8,128)}), f32[1,4,32,4,64,128]{5,4,3,1,0,2:T(8,128)}, u32[]{:S(2)}, u32[]{:S(2)}) async-start(f32[1,4,32,4,64,128]{5,4,3,1,0,2:T(8,128)} %copy.120), calls=%async_computation.2 | async-start | bytes 33554432 | tf_op jit(solution)/shard_map/all_to_all | solution.py:230
  714.3 302.4 %all-reduce.32.cloned.1.call-start = ((), (), s32[]{:S(2)}) async-start(), calls=%async_computation.6 | async-start | bytes 150528
  721.9 448.7 %reduce-scatter.4.cloned.1.call-start = ((), (), s32[]{:S(2)}) async-start(), calls=%async_computation.5 | async-start | bytes 5898240
  734.2 450.7 %copy-start.31 = (s32[128]{0:T(128)S(1)}, s32[128]{0:T(128)}, u32[]{:S(2)}) copy-start(s32[128]{0:T(128)} %param.24) | copy-start | bytes 1540
  (38 other events, 303.2 us)
Sparse Core Ops, SparseCore 0:
  722.0 294.5 all-reduce.31
  1020.2 150.2 reduce-scatter.3
where the time goes:
time: 1250 us; the launch traced here: 1240 us
  waiting for transfers between devices  435 us (35%)
  blocking collectives  286 us (23%)
  local copies, waits for them, and re-layouts  227 us (18%)
  matrix products  194 us (16%)
  other arithmetic  59.2 us (5%)
  starting transfers between devices  22.1 us (2%)
  between operations  17.8 us (1%)
    unnamed x4, waiting for transfers between devices  429 us
    unnamed x1, blocking collectives  148 us
    dot_general x24, matrix products, group_mix(): jnp.einsum('kts,skp->tkp', weights, x_rows, precision=lax.Precision.HIGHEST)  70.7 us
    dot_general x32, matrix products, group_mix(): jnp.einsum('tdn,dkpn->tkp', c_masked, start_state, precision=lax.Precisio...  69.3 us
    all_gather x1, blocking collectives, shards(): lax.all_gather(norm_gain, 'fsdp', axis=0, tiled=True)  64.8 us
    squeeze x56, local copies, waits for them, and re-layouts, mixer_forward(): lax.map(jax.checkpoint(group_mix), (c_all, b_all, x_heads, by_group(step_...  54.8 us
    unnamed x132, local copies, waits for them, and re-layouts  32.2 us
    all_gather x1, blocking collectives, shards(): lax.all_gather(conv_bias, 'fsdp', axis=0, tiled=True)  30.6 us
  transfers between devices with their start and end apart: 6, of which 3 were waited for; matrix products, arithmetic and copies ran while one was open for 9% of the time, Pallas kernels for 0%

commit v1 on v0

v1 whole, which is shorter than its diff:
```python
import functools

import jax
import jax.numpy as jnp
from jax import lax
from jax.experimental import pallas as pl
from jax.experimental.pallas import tpu as pltpu
from jax.sharding import PartitionSpec as P

GROUP = 16
H = 128
P_SIZE = 64
N = 128
G = 8
GS = 2048
DI = H * P_SIZE
GN = G * N

CH = 256
HC = CH // P_SIZE
F32 = jnp.float32
BF16 = jnp.bfloat16
NN = (((1,), (0,)), ((), ()))
NT = (((1,), (1,)), ((), ()))


def advantages(rewards, resp_prompt, prompt_count):
    member = (resp_prompt[:, None] == jnp.arange(prompt_count, dtype=jnp.int32)[None, :]).astype(
        jnp.float32
    )
    group_mean = jnp.dot(rewards, member, precision=lax.Precision.HIGHEST) / GROUP
    centred = rewards - jnp.dot(member, group_mean, precision=lax.Precision.HIGHEST)
    spread = jnp.sqrt(jnp.dot(centred * centred, member, precision=lax.Precision.HIGHEST) / GROUP)
    return centred / jnp.dot(member, jnp.maximum(spread, 0.8), precision=lax.Precision.HIGHEST)


def dot(a, b, dims=NN):
    return lax.dot_general(a, b, dims, preferred_element_type=F32)


def split2(a):
    hi = a.astype(BF16)
    return hi, (a - hi.astype(F32)).astype(BF16)


def split3(a):
    hi = a.astype(BF16)
    rest = a - hi.astype(F32)
    mid = rest.astype(BF16)
    return hi, mid, (rest - mid.astype(F32)).astype(BF16)


def dot3(a, b, dims=NN):
    ah, al = split2(a)
    bh, bl = split2(b)
    return dot(ah, bh, dims) + dot(ah, bl, dims) + dot(al, bh, dims)


def exact_left(mask, table):
    hi, mid, lo = split3(table)
    return dot(mask, hi) + dot(mask, mid) + dot(mask, lo)


def colsum(a):
    return jnp.sum(a, axis=0, keepdims=True)


def mixer_kernel(
    dims,
    prompt_ref,
    adv_ref,
    recv_ref,
    tails_ref,
    wv_ref,
    hv_ref,
    states_ref,
    out_ref,
    dstate_ref,
    dtail_ref,
    wg_ref,
    st,
    acc,
    uext,
    co,
    dco,
    ybuf,
    sc,
    sct,
    cmh,
    cml,
    relt,
    rel3,
    se3,
    dred,
    dsc,
    dcc,
    sems,
    out_sem,
):
    rows, docs, chans, inner, heads, groups, fcount, share_rows = dims
    nf = CH // share_rows
    k = pl.program_id(0)
    inner_chunks = inner // CH
    all_chunks = chans // CH
    zoff, upoff, moff = chans, chans + inner, chans + 2 * inner
    b_off, c_off = inner, inner + groups * N

    copies = [
        pltpu.make_async_copy(states_ref.at[:, prompt_ref[k * docs + d]], st.at[d], sems.at[d])
        for d in range(docs)
    ]
    for copy in copies:
        copy.start()

    @pl.when(k == 0)
    def _():
        wg_ref[...] = jnp.zeros_like(wg_ref)
        uext[...] = jnp.zeros_like(uext)

        def clear(f, carry):
            acc[f] = jnp.zeros(acc.shape[1:], F32)
            return carry

        lax.fori_loop(0, fcount, clear, 0)

    meta = recv_ref[0, :, moff : moff + 128].astype(F32)
    lens = [meta[0:1, 96 + d : 97 + d] for d in range(docs)]
    tcol = lax.broadcasted_iota(jnp.int32, (rows, 1), 0).astype(F32)
    trow = lax.broadcasted_iota(jnp.int32, (1, rows), 1).astype(F32)
    doc_col, doc_row = jnp.zeros_like(tcol), jnp.zeros_like(trow)
    start_col, start_row = jnp.zeros_like(tcol), jnp.zeros_like(trow)
    begin = jnp.zeros((1, 1), F32)
    for d in range(docs - 1):
        begin = begin + lens[d]
        doc_col = doc_col + jnp.where(tcol >= begin, 1.0, 0.0)
        doc_row = doc_row + jnp.where(trow >= begin, 1.0, 0.0)
        start_col = jnp.where(tcol >= begin, begin, start_col)
        start_row = jnp.where(trow >= begin, begin, start_row)
    off_col, off_row = tcol - start_col, trow - start_row
    wtok = jnp.zeros_like(tcol)
    for d in range(docs):
        wtok = wtok + jnp.where(
            doc_col == d, adv_ref[k * docs + d] * (rows / (docs * lens[d])), 0.0
        )
    same = doc_col == doc_row
    causal = same & (tcol >= trow)
    causal_t = same & (trow >= tcol)

    ext_row = lax.broadcasted_iota(jnp.int32, (1, 2 * rows), 1).astype(F32)
    ext_col = lax.broadcasted_iota(jnp.int32, (rows + 16, 1), 0).astype(F32)
    shift, shift_t = [], []
    for j in (1, 2, 3):
        src_col = jnp.where(off_col >= j, tcol - j, rows + doc_col * 4 + (3 - j) + off_col)
        src_row = jnp.where(off_row >= j, trow - j, rows + doc_row * 4 + (3 - j) + off_row)
        shift.append(jnp.where(src_col == ext_row, 1.0, 0.0).astype(BF16))
        shift_t.append(jnp.where(src_row == ext_col, 1.0, 0.0).astype(BF16))
    shift = jnp.concatenate(shift, axis=0)
    shift_t = jnp.concatenate(shift_t, axis=1)

    uext[0:rows, :] = recv_ref[0, :, 0:chans]
    uext[rows : rows + 16, :] = tails_ref[0]

    def conv(cs):
        u = uext[:, pl.ds(cs, CH)]
        lag = dot(shift, u)
        taps = [u[0:rows].astype(F32)] + [lag[i * rows : (i + 1) * rows] for i in range(3)]
        w = [wv_ref[3 - j : 4 - j, pl.ds(cs, CH)] for j in range(4)]
        pre = wv_ref[4:5, pl.ds(cs, CH)] + sum(w[j] * taps[j] for j in range(4))
        return pre, taps, w

    def conv_step(i, carry):
        cs = pl.multiple_of(i * CH, CH)
        pre, _, _ = conv(cs)
        co[:, pl.ds(cs, CH)] = pre * jax.nn.sigmoid(pre)
        return carry

    lax.fori_loop(0, all_chunks, conv_step, 0)

    for g in range(groups):
        bg = co[:, b_off + g * N : b_off + (g + 1) * N]
        cg = co[:, c_off + g * N : c_off + (g + 1) * N]
        sc[g] = dot3(cg, bg, NT)
        sct[g] = dot3(bg, cg, NT)
        hi, lo = split2(cg)
        zero = jnp.zeros_like(hi)
        for d in range(docs):
            cmh[g, :, d * N : (d + 1) * N] = jnp.where(doc_col == d, hi, zero)
            cml[g, :, d * N : (d + 1) * N] = jnp.where(doc_col == d, lo, zero)
        dsc[g] = jnp.zeros((rows, rows), F32)
        dcc[g] = jnp.zeros((rows, N), F32)
    dred[...] = jnp.zeros_like(dred)

    dt_pre = meta[:, 0:32] + meta[:, 32:64] + meta[:, 64:96] + hv_ref[0:1, :]
    tail_exp = jnp.exp(-jnp.abs(dt_pre))
    step = jnp.maximum(dt_pre, 0.0) + jnp.log1p(tail_exp)
    rate = -jnp.exp(hv_ref[1:2, :])
    dec = step * rate
    rel = exact_left(jnp.where(causal, 1.0, 0.0).astype(BF16), dec)
    relt[...] = rel.T
    rel3[...] = jnp.concatenate(split3(rel), axis=1)
    se3[0:rows, :] = jnp.concatenate(split3(step), axis=1)
    se3[rows : 2 * rows, :] = jnp.concatenate(split3(jnp.exp(rel)), axis=1)

    def head_onehot(c, width):
        r = lax.broadcasted_iota(jnp.int32, (3 * heads, HC * width), 0)
        r = jnp.where(r >= 2 * heads, r - 2 * heads, jnp.where(r >= heads, r - heads, r))
        lane = lax.broadcasted_iota(jnp.int32, (3 * heads, HC * width), 1)
        return jnp.where(r == c * HC + lane // width, 1.0, 0.0).astype(BF16)

    lane_head = lax.broadcasted_iota(jnp.int32, (1, CH), 1) // P_SIZE

    def block_diag(a):
        zero = jnp.zeros_like(a)
        return jnp.concatenate([jnp.where(lane_head == h, a, zero) for h in range(HC)], axis=0)

    def chunk_tables(c):
        expand = dot(se3[...], head_onehot(c, P_SIZE))
        colb = dot(rel3[...], head_onehot(c, rows))
        rowb = [relt[pl.ds(c * HC + h, 1), :] for h in range(HC)]
        return expand[0:rows], expand[rows : 2 * rows], colb, rowb

    def state_of(d, c):
        return st[d, pl.ds(c * nf, nf)].reshape(CH, N)

    for copy in copies:
        copy.wait()

    def forward_step(c, carry):
        s1, s2 = carry
        cs = pl.multiple_of(c * CH, CH)
        g = c // (inner_chunks // groups)
        stepx, ex, colb, rowb = chunk_tables(c)
        x = co[:, pl.ds(cs, CH)]
        xh, xl = split2(x * stepx)
        score = sc[g]
        w = jnp.concatenate(
            [
                jnp.exp(jnp.where(causal, colb[:, h * rows : (h + 1) * rows] - rowb[h], -1e30))
                * score
                for h in range(HC)
            ],
            axis=1,
        )
        wh, wl = split2(w)
        bh, bl = block_diag(xh), block_diag(xl)
        within = dot(wh, bh) + dot(wh, bl) + dot(wl, bh)
        carried = jnp.zeros((rows, CH), F32)
        for d in range(docs):
            state = state_of(d, c)
            carried = carried + dot(cmh[g, :, d * N : (d + 1) * N], state, NT)
            carried = carried + dot(cml[g, :, d * N : (d + 1) * N], state, NT)
        y = within + ex * carried + wv_ref[6:7, pl.ds(cs, CH)] * x
        ybuf[:, pl.ds(cs, CH)] = y
        z = recv_ref[0, :, pl.ds(zoff + cs, CH)].astype(F32)
        up = recv_ref[0, :, pl.ds(upoff + cs, CH)].astype(F32)
        v = y * (z * jax.nn.sigmoid(z))
        p1 = v * v
        p2 = up * wv_ref[5:6, pl.ds(cs, CH)] * v
        return s1 + p1[:, :128] + p1[:, 128:], s2 + p2[:, :128] + p2[:, 128:]

    zeros = jnp.zeros((rows, 128), F32)
    s1, s2 = lax.fori_loop(0, inner_chunks, forward_step, (zeros, zeros))
    inv = lax.rsqrt(jnp.sum(s1, axis=1, keepdims=True) / GS + 1e-05)
    mean2 = jnp.sum(s2, axis=1, keepdims=True) * wtok / GS
    coef = inv * inv * inv * mean2

    def backward_step(c, carry):
        cs = pl.multiple_of(c * CH, CH)
        g = c // (inner_chunks // groups)
        stepx, ex, colb, rowb = chunk_tables(c)
        x = co[:, pl.ds(cs, CH)]
        y = ybuf[:, pl.ds(cs, CH)]
        z = recv_ref[0, :, pl.ds(zoff + cs, CH)].astype(F32)
        up = recv_ref[0, :, pl.ds(upoff + cs, CH)].astype(F32)
        skip = wv_ref[6:7, pl.ds(cs, CH)]
        sg = jax.nn.sigmoid(z)
        sz = z * sg
        v = y * sz
        dn = up * (wtok * inv)
        wg_ref[5:6, pl.ds(cs, CH)] += colsum(dn * v)
        dv = dn * wv_ref[5:6, pl.ds(cs, CH)] - v * coef
        dy = dv * sz
        out_ref[0, :, pl.ds(chans + cs, CH)] = (dv * y * (sg * (1.0 + z * (1.0 - sg)))).astype(
            BF16
        )
        xs = x * stepx
        xh, xl = split2(xs)
        dyh, dyl = split2(dy)
        bh, bl = block_diag(xh), block_diag(xl)
        dm = dot(dyh, bh, NT) + dot(dyh, bl, NT) + dot(dyl, bh, NT)
        score_t = sct[g]
        total = dsc[g]
        wt = []
        for h in range(HC):
            gap = colb[:, h * rows : (h + 1) * rows] - rowb[h]
            total = total + jnp.exp(jnp.where(causal, gap, -1e30)) * dm[:, h * rows : (h + 1) * rows]
            wt.append(jnp.exp(jnp.where(causal_t, -gap, -1e30)) * score_t)
        dsc[g] = total
        wh, wl = split2(jnp.concatenate(wt, axis=1))
        dh, dl = block_diag(dyh), block_diag(dyl)
        dxs = dot(wh, dh) + dot(wh, dl) + dot(wl, dh)
        dco[:, pl.ds(cs, CH)] = stepx * dxs + skip * dy
        wg_ref[6:7, pl.ds(cs, CH)] += colsum(dy * x)
        both = jnp.concatenate([dy * (y - skip * x) - xs * dxs, dxs * x], axis=0)
        pick = jnp.where(
            lax.broadcasted_iota(jnp.int32, (CH, heads), 0) // P_SIZE + c * HC
            == lax.broadcasted_iota(jnp.int32, (CH, heads), 1),
            1.0,
            0.0,
        ).astype(BF16)
        b1, b2, b3 = split3(both)
        dred[...] += dot(b1, pick) + dot(b2, pick) + dot(b3, pick)
        q = ex * dy
        qh, ql = split2(q)
        qth, qtl = split2(q.T)
        ch, cl = cmh[g], cml[g]
        ds_all = dot(qth, ch) + dot(qtl, ch) + dot(qth, cl)
        back = jnp.zeros((rows, N), F32)
        for d in range(docs):
            p = prompt_ref[k * docs + d]
            acc[pl.ds(c * nf, nf), p] += ds_all[:, d * N : (d + 1) * N].reshape(nf, share_rows, N)
            state = state_of(d, c)
            back = back + jnp.where(doc_col == d, dot(qh, state) + dot(ql, state), 0.0)
        dcc[g] += back
        return carry

    lax.fori_loop(0, inner_chunks, backward_step, 0)

    @pl.when(k == pl.num_programs(0) - 1)
    def _():
        pltpu.make_async_copy(acc, dstate_ref, out_sem).start()

    for g in range(groups):
        bg = co[:, b_off + g * N : b_off + (g + 1) * N]
        cg = co[:, c_off + g * N : c_off + (g + 1) * N]
        dco[:, c_off + g * N : c_off + (g + 1) * N] = dot3(dsc[g], bg) + dcc[g]
        dco[:, b_off + g * N : b_off + (g + 1) * N] = dot3(dsc[g].T, cg)

    ddec = exact_left(jnp.where(causal_t, 1.0, 0.0).astype(BF16), dred[0:rows])
    ddt = (dred[rows : 2 * rows] + ddec * rate) * jax.nn.sigmoid(dt_pre)
    wg_ref[7:8, 0:heads] += colsum(ddt)
    wg_ref[8:9, 0:heads] += colsum(ddec * dec)
    out_ref[0, :, chans + inner :] = jnp.concatenate(
        list(split3(ddt)) + [jnp.zeros((rows, 128 - 3 * heads), BF16)], axis=1
    )

    def conv_back(i, carry):
        cs = pl.multiple_of(i * CH, CH)
        pre, taps, w = conv(cs)
        sg = jax.nn.sigmoid(pre)
        dpre = dco[:, pl.ds(cs, CH)] * (sg * (1.0 + pre * (1.0 - sg)))
        for j in range(4):
            wg_ref[3 - j : 4 - j, pl.ds(cs, CH)] += colsum(dpre * taps[j])
        wg_ref[4:5, pl.ds(cs, CH)] += colsum(dpre)
        hi, lo = split2(jnp.concatenate([w[j] * dpre for j in (1, 2, 3)], axis=0))
        du = dot(shift_t, hi) + dot(shift_t, lo)
        out_ref[0, :, pl.ds(cs, CH)] = (w[0] * dpre + du[0:rows]).astype(BF16)
        dtail_ref[0, :, pl.ds(cs, CH)] = du[rows : rows + 16]
        return carry

    lax.fori_loop(0, all_chunks, conv_back, 0)

    @pl.when(k == pl.num_programs(0) - 1)
    def _():
        pltpu.make_async_copy(acc, dstate_ref, out_sem).wait()


def run_mixer(prompts, adv, recv, tails, wv, hv, states, docs):
    blocks, rows, width = recv.shape
    chans = wv.shape[1]
    fcount, prompt_count, share_rows, _ = states.shape
    inner = fcount * share_rows
    heads = inner // P_SIZE
    groups = (chans - inner) // (2 * N)
    dims = (rows, docs, chans, inner, heads, groups, fcount, share_rows)
    out_width = chans + inner + 128
    smem = pl.BlockSpec(memory_space=pltpu.SMEM)
    hbm = pl.BlockSpec(memory_space=pl.ANY)
    return pl.pallas_call(
        functools.partial(mixer_kernel, dims),
        grid=(blocks,),
        in_specs=[
            smem,
            smem,
            pl.BlockSpec((1, rows, width), lambda i: (i, 0, 0)),
            pl.BlockSpec((1, 16, chans), lambda i: (i, 0, 0)),
            pl.BlockSpec(wv.shape, lambda i: (0, 0)),
            pl.BlockSpec(hv.shape, lambda i: (0, 0)),
            hbm,
        ],
        out_specs=[
            pl.BlockSpec((1, rows, out_width), lambda i: (i, 0, 0)),
            hbm,
            pl.BlockSpec((1, 16, chans), lambda i: (i, 0, 0)),
            pl.BlockSpec((16, chans), lambda i: (0, 0)),
        ],
        out_shape=[
            jax.ShapeDtypeStruct((blocks, rows, out_width), BF16),
            jax.ShapeDtypeStruct(states.shape, F32),
            jax.ShapeDtypeStruct((blocks, 16, chans), F32),
            jax.ShapeDtypeStruct((16, chans), F32),
        ],
        scratch_shapes=[
            pltpu.VMEM((docs, fcount, share_rows, N), BF16),
            pltpu.VMEM(states.shape, F32),
            pltpu.VMEM((2 * rows, chans), BF16),
            pltpu.VMEM((rows, chans), F32),
            pltpu.VMEM((rows, chans), F32),
            pltpu.VMEM((rows, inner), F32),
            pltpu.VMEM((groups, rows, rows), F32),
            pltpu.VMEM((groups, rows, rows), F32),
            pltpu.VMEM((groups, rows, docs * N), BF16),
            pltpu.VMEM((groups, rows, docs * N), BF16),
            pltpu.VMEM((heads, rows), F32),
            pltpu.VMEM((rows, 3 * heads), BF16),
            pltpu.VMEM((2 * rows, 3 * heads), BF16),
            pltpu.VMEM((2 * rows, heads), F32),
            pltpu.VMEM((groups, rows, rows), F32),
            pltpu.VMEM((groups, rows, N), F32),
            pltpu.SemaphoreType.DMA((docs,)),
            pltpu.SemaphoreType.DMA,
        ],
        compiler_params=pltpu.CompilerParams(
            dimension_semantics=("arbitrary",), vmem_limit_bytes=60 * 1024 * 1024
        ),
        cost_estimate=pl.CostEstimate(
            flops=20_000_000_000, bytes_accessed=30_000_000, transcendentals=10_000_000
        ),
        name="mixer",
    )(prompts, adv, recv, tails, wv, hv, states)


def shards(
    xbc,
    zgate,
    dt_raw,
    prompt_states,
    conv_tails,
    resp_prompt,
    resp_lengths,
    rewards,
    upstream,
    conv_weight,
    conv_bias,
    dt_bias,
    a_log,
    d_skip,
    norm_gain,
):
    dp_count = lax.axis_size("dp")
    fsdp_count = lax.axis_size("fsdp")
    dp_at = lax.axis_index("dp")
    fsdp_at = lax.axis_index("fsdp")
    docs = resp_lengths.shape[1]
    rows = xbc.shape[0]
    prompt_count, head_share = prompt_states.shape[:2]
    chan_share = conv_tails.shape[2]
    inner = DI // dp_count
    gn = GN // dp_count
    chans = inner + 2 * gn
    heads = H // dp_count

    def by_dest(a):
        return a.reshape(rows, dp_count, -1).transpose(1, 0, 2)

    hi = lax.reduce_precision(dt_raw, 8, 7)
    rest = dt_raw - hi
    mid = lax.reduce_precision(rest, 8, 7)
    low = rest - mid
    lens_cols = jnp.broadcast_to(
        resp_lengths.astype(BF16).reshape(1, 1, docs), (dp_count, rows, docs)
    )
    sent = jnp.concatenate(
        [
            by_dest(xbc[:, :DI]),
            by_dest(xbc[:, DI : DI + GN]),
            by_dest(xbc[:, DI + GN :]),
            by_dest(zgate),
            by_dest(upstream),
            by_dest(hi.astype(BF16)),
            by_dest(mid.astype(BF16)),
            by_dest(low.astype(BF16)),
            lens_cols,
            jnp.zeros((dp_count, rows, 128 - 3 * heads - docs), BF16),
        ],
        axis=2,
    )
    recv = lax.all_to_all(sent, "dp", split_axis=0, concat_axis=0, tiled=True)

    states = lax.all_gather(
        prompt_states.reshape(prompt_count, head_share * P_SIZE, N), "fsdp", axis=0
    )

    chan_w = conv_weight.shape[1]
    flat = jnp.concatenate(
        [conv_weight.reshape(-1), conv_bias, norm_gain, dt_bias, a_log, d_skip]
    )
    flat = lax.all_gather(flat, "fsdp", axis=0)
    conv_all = flat[:, : 5 * chan_w].reshape(fsdp_count, 5, chan_w).transpose(1, 0, 2)
    conv_all = conv_all.reshape(5, fsdp_count * chan_w)
    gain_w = norm_gain.shape[0]
    gain_all = flat[:, 5 * chan_w : 5 * chan_w + gain_w].reshape(-1)
    per_head = flat[:, 5 * chan_w + gain_w :].reshape(fsdp_count, 3, -1).transpose(1, 0, 2)
    per_head = lax.dynamic_slice_in_dim(per_head.reshape(3, H), dp_at * heads, heads, 1)

    def own_channels(a):
        return jnp.concatenate(
            [
                lax.dynamic_slice_in_dim(a, dp_at * inner, inner, a.ndim - 1),
                lax.dynamic_slice_in_dim(a, DI + dp_at * gn, gn, a.ndim - 1),
                lax.dynamic_slice_in_dim(a, DI + GN + dp_at * gn, gn, a.ndim - 1),
            ],
            axis=-1,
        )

    def pad_row(a):
        return jnp.pad(a, (0, chans - inner))[None]

    wv = jnp.concatenate(
        [
            own_channels(conv_all),
            pad_row(lax.dynamic_slice_in_dim(gain_all, dp_at * inner, inner)),
            pad_row(jnp.repeat(per_head[2], P_SIZE)),
            jnp.zeros((1, chans), F32),
        ]
    )
    hv = jnp.concatenate([per_head[:2], jnp.zeros((6, heads), F32)])

    holders = jnp.arange(dp_count, dtype=jnp.int32) * fsdp_count + fsdp_at
    prompts = resp_prompt.reshape(-1, docs)[holders].reshape(-1)
    adv = advantages(rewards, resp_prompt, prompt_count)
    adv = adv.reshape(-1, docs)[holders].reshape(-1)

    tails = lax.all_gather(conv_tails, ("dp", "fsdp"), axis=0)
    tails = tails.transpose(1, 2, 0, 3).reshape(prompt_count, 3, -1)
    tails = jnp.pad(own_channels(tails), ((0, 0), (0, 1), (0, 0)))
    tails = tails[prompts].reshape(dp_count, docs * 4, chans)

    out, dstate, dtail, wg = run_mixer(prompts, adv, recv, tails, wv, hv, states, docs)

    grad_states = lax.psum_scatter(dstate, "fsdp", scatter_dimension=0, tiled=False)
    grad_states = grad_states.reshape(prompt_count, head_share, P_SIZE, N)

    back = lax.all_to_all(out, "dp", split_axis=0, concat_axis=0, tiled=True)

    def home(lo, width):
        return back[:, :, lo : lo + width].transpose(1, 0, 2).reshape(rows, dp_count * width)

    grad_x = jnp.concatenate([home(0, inner), home(inner, gn), home(inner + gn, gn)], axis=1)
    grad_z = home(chans, inner)
    parts = [home(chans + inner + i * heads, heads).astype(F32) for i in range(3)]
    grad_dt = parts[0] + parts[1] + parts[2]

    onehot = (jnp.arange(prompt_count, dtype=jnp.int32)[:, None] == prompts[None, :]).astype(F32)
    dtail = dtail.reshape(dp_count * docs, 4, chans)[:, :3].reshape(dp_count * docs, 3 * chans)
    dtail = jnp.dot(onehot, dtail, precision=lax.Precision.HIGHEST)

    def spread(a, lead):
        full = jnp.zeros((lead, DI + 2 * GN), F32)
        full = lax.dynamic_update_slice(full, a[:, :inner], (0, dp_at * inner))
        full = lax.dynamic_update_slice(full, a[:, inner : inner + gn], (0, DI + dp_at * gn))
        return lax.dynamic_update_slice(full, a[:, inner + gn :], (0, DI + GN + dp_at * gn))

    tail_full = spread(dtail.reshape(prompt_count * 3, chans), prompt_count * 3)
    tail_full = tail_full.reshape(prompt_count * 3, dp_count, fsdp_count, chan_share)
    tail_full = tail_full.transpose(2, 1, 0, 3).reshape(fsdp_count, -1)
    conv_full = spread(wg[:5], 5).reshape(5, fsdp_count, chan_w).transpose(1, 0, 2)
    gain_full = lax.dynamic_update_slice(jnp.zeros((DI,), F32), wg[5, :inner], (dp_at * inner,))
    skip_grad = jnp.sum(wg[6, :inner].reshape(heads, P_SIZE), axis=1)
    head_grad = jnp.stack([wg[7, :heads], wg[8, :heads], skip_grad])
    head_full = lax.dynamic_update_slice(jnp.zeros((3, H), F32), head_grad, (0, dp_at * heads))
    head_full = head_full.reshape(3, fsdp_count, -1).transpose(1, 0, 2)
    payload = jnp.concatenate(
        [
            tail_full,
            conv_full.reshape(fsdp_count, -1),
            gain_full.reshape(fsdp_count, -1),
            head_full.reshape(fsdp_count, -1),
        ],
        axis=1,
    )
    summed = lax.psum(lax.psum_scatter(payload, "fsdp", scatter_dimension=0, tiled=False), "dp")
    tail_size = prompt_count * 3 * chan_share
    grad_tails = lax.dynamic_slice_in_dim(summed, dp_at * tail_size, tail_size)
    grad_tails = grad_tails.reshape(prompt_count, 3, chan_share)
    rest = summed[dp_count * tail_size :]
    grad_conv = rest[: 5 * chan_w].reshape(5, chan_w)
    rest = rest[5 * chan_w :]
    per = dt_bias.shape[0]
    return (
        grad_x,
        grad_z,
        grad_dt,
        grad_states,
        grad_tails,
        grad_conv[:4],
        grad_conv[4],
        rest[gain_w : gain_w + per],
        rest[gain_w + per : gain_w + 2 * per],
        rest[gain_w + 2 * per : gain_w + 3 * per],
        rest[:gain_w],
    )


def solution(mesh):
    return jax.shard_map(
        shards,
        mesh=mesh,
        in_specs=(
            P(("dp", "fsdp"), None),
            P(("dp", "fsdp"), None),
            P(("dp", "fsdp"), None),
            P(None, ("dp", "fsdp"), None, None),
            P(None, None, ("dp", "fsdp")),
            P(),
            P(("dp", "fsdp"), None),
            P(),
            P(("dp", "fsdp"), None),
            P(None, "fsdp"),
            P("fsdp"),
            P("fsdp"),
            P("fsdp"),
            P("fsdp"),
            P("fsdp"),
        ),
        out_specs=(
            P(("dp", "fsdp"), None),
            P(("dp", "fsdp"), None),
            P(("dp", "fsdp"), None),
            P(None, ("dp", "fsdp"), None, None),
            P(None, None, ("dp", "fsdp")),
            P(None, "fsdp"),
            P("fsdp"),
            P("fsdp"),
            P("fsdp"),
            P("fsdp"),
            P("fsdp"),
        ),
        check_vma=False,
    )
```

time: 1250 us -> 554 us (0.44)
  blocking collectives: 286 us -> 77.3 us
  matrix products: 194 us -> 1.19 us
  waiting for transfers between devices: 435 us -> 244 us
  local copies, waits for them, and re-layouts: 227 us -> 82.2 us
  Pallas kernels: 0 us -> 107 us
  other arithmetic: 59.2 us -> 13.6 us
    unnamed x4 -> x7, waiting for transfers between devices: 429 us -> 81.9 us
    dot_general x92 -> x1, matrix products: 193 us -> 0.28 us  [shards(): dtail = jnp.dot(onehot, dtail, precision=lax.Precision.HIGHEST)]
    unnamed x1 -> x0, blocking collectives: 148 us -> none
    pallas_call x0 -> x1, Pallas kernels: none -> 107 us  [run_mixer(): pl.pallas_call(functools.partial(mixer_kernel, dims), grid=(blocks,), in_...]
    reduce_scatter x0 -> x1, waiting for transfers between devices: none -> 93.5 us  [shards(): lax.psum_scatter(dstate, 'fsdp', scatter_dimension=0, tiled=False)]
    squeeze x56 -> x1, local copies, waits for them, and re-layouts: 54.8 us -> 0.01 us  [shards(): per_head[2]]
    all_gather x3 -> x1, blocking collectives: 126 us -> 77.3 us  [shards(): tails = lax.all_gather(conv_tails, ('dp', 'fsdp'), axis=0)]
    reshape x15 -> x27, local copies, waits for them, and re-layouts: 51.9 us -> 18.2 us  [the longest x8 11.6 us: by_dest(): return a.reshape(rows, dp_count, -1).transpose(1, 0, 2)]
  transfers between devices with their start and end apart: 6 -> 7, of which waited for: 3 -> 5; matrix products, arithmetic and copies ran while one was open for 9% -> 14% of each run, Pallas kernels for 0% -> 0%
where the time goes in v1:
time: 554 us; the launch traced here: 552 us
  waiting for transfers between devices  244 us (44%)
  Pallas kernels  107 us (19%)
  local copies, waits for them, and re-layouts  82.2 us (15%)
  blocking collectives  77.3 us (14%)
  between operations  15.1 us (3%)
  other arithmetic  13.6 us (2%)
  starting transfers between devices  11.1 us (2%)
    pallas_call x1, Pallas kernels, run_mixer(): pl.pallas_call(functools.partial(mixer_kernel, dims), grid=(blocks,), in_...  107 us
    reduce_scatter x1, waiting for transfers between devices, shards(): lax.psum_scatter(dstate, 'fsdp', scatter_dimension=0, tiled=False)  93.5 us
    unnamed x7, waiting for transfers between devices  81.9 us
    all_gather x1, blocking collectives, shards(): tails = lax.all_gather(conv_tails, ('dp', 'fsdp'), axis=0)  77.3 us
    psum x1, waiting for transfers between devices, shards(): lax.psum(lax.psum_scatter(payload, 'fsdp', scatter_dimension=0, tiled=Fal...  25.7 us
    all_to_all x1, waiting for transfers between devices, shards(): back = lax.all_to_all(out, 'dp', split_axis=0, concat_axis=0, tiled=True)  24.3 us
    unnamed x37, local copies, waits for them, and re-layouts  23.4 us
    all_gather x1, waiting for transfers between devices, shards(): lax.all_gather(prompt_states.reshape(prompt_count, head_share * P_SIZE, N...  19 us
  transfers between devices with their start and end apart: 7, of which 5 were waited for; matrix products, arithmetic and copies ran while one was open for 14% of the time, Pallas kernels for 0%

profile of v1, /device:TPU:0, one launch (start us, length us, event | category | flops | bytes accessed | tf_op | source)
XLA Modules:
  0.0 552.2 jit_solution(3779887310922925709)
XLA Ops:
  14.2 1.7 copy-done
  17.6 2.4 copy.115
  20.0 2.9 copy.85
  22.9 4.1 copy.90
  27.0 3.9 copy.91
  31.0 4.1 copy.92
  35.0 4.1 copy.93
  39.2 11.4 %concatenate.24 = bf16[4,128,6784]{2,1,0:T(8,128)(2,1)} concatenate(bf16[4,128,2048]{2,1,0:T(8,128)(2,1)S(1)} %bitcast.116, bf16[4,128,256]{2,1,0:T(8,128)(2,1)S(1)} %bitcast.130, bf16[4,128,256]{2,1,0:T(8,128)(2,1)S(1)} %bitcast.131, bf16[4,128,2048]{2,1,0:T(8,128)(2,1)} %bitcast.117, bf16[4,128,2048]{2,1,0:T(8,128)(2,1)} %bitcast.118, bf16[4,128,32]{2,1,0:T(8,128)(2,1)S(1)} %bitcast.138, ...), dimensions={2} | concatenate | bytes 13893632 | tf_op jit(solution)/shard_map/concatenate | solution.py:473
  50.6 5.6 %all-to-all-start = ((bf16[4,128,6784]{2,1,0:T(8,128)(2,1)}), bf16[4,128,6784]{2,1,0:T(8,128)(2,1)}, u32[]{:S(2)}, u32[]{:S(2)}) async-start(bf16[4,128,6784]{2,1,0:T(8,128)(2,1)} %concatenate.24), calls=%async_computation | async-start | bytes 13893632 | tf_op jit(solution)/shard_map/all_to_all | solution.py:488
  57.6 77.3 %all-gather = bf16[256,3,320]{2,0,1:T(8,128)(2,1)S(1)} all-gather(bf16[8,3,320]{2,0,1:T(8,128)(2,1)S(1)} %copy-done.3), channel_id=2, replica_groups=mesh['dp'=4,'fsdp'=8] {'dp','fsdp'}, dimensions={0}, use_global_device_ids=true | all-gather | bytes 506880 | tf_op jit(solution)/shard_map/all_gather | solution.py:534
  143.0 19.0 %all-gather.4.cloned.1.call-done.states_ref = bf16[8,8,256,128]{3,2,1,0:T(8,128)(2,1)} async-done(((bf16[1,8,256,128]{3,2,1,0:T(8,128)(2,1)}), bf16[8,8,256,128]{3,2,1,0:T(8,128)(2,1)}) %all-gather.4.cloned.1.call-update) | async-done | bytes 4194320 | tf_op jit(solution)/shard_map/all_gather | solution.py:490
  161.9 107.5 %mixer.1 = (bf16[4,128,4736]{2,1,0:T(8,128)(2,1)}, f32[8,8,256,128]{3,2,1,0:T(8,128)}, f32[4,16,2560]{2,1,0:T(8,128)}, f32[16,2560]{1,0:T(8,128)}) custom-call(s32[16]{0:T(128)} %reshape.198.prompt_ref, f32[16]{0:T(128)} %reshape.200.adv_ref, bf16[4,128,6784]{2,1,0:T(8,128)(2,1)} %all-to-all-done.recv_ref, bf16[4,16,2560]{2,1,0:T(8,128)(2,1)} %reshape.211.tails_ref, ...), custom_call_target="tpu_custom_call" | custom-call | flops 20000000000 | bytes 30000000 | tf_op jit(solution)/shard_map/mixer/pallas_call | solution.py:379
  277.0 80.6 %all-reduce.14.cloned.1.call-done = f32[8,38192]{1,0:T(8,128)} async-done(((f32[8,38192]{1,0:T(8,128)}), f32[8,38192]{1,0:T(8,128)}) %all-reduce.14.cloned.1.call-update) | async-done | bytes 1222160
  357.5 3.0 dynamic-slice_reduce_fusion
  361.2 5.3 all-to-all-start.1
  366.5 25.7 %all-reduce.10.cloned.1.call-done = f32[38192]{0:T(1024)} async-done(((f32[38192]{0:T(1024)}), f32[38192]{0:T(1024)}) %all-reduce.10.cloned.1.call-update) | async-done | bytes 152784 | tf_op jit(solution)/shard_map/psum | solution.py:582
  399.1 24.3 %all-to-all-done.1 = bf16[4,128,4736]{2,1,0:T(8,128)(2,1)} async-done(((bf16[4,128,4736]{2,1,0:T(8,128)(2,1)}), bf16[4,128,4736]{2,1,0:T(8,128)(2,1)}, u32[]{:S(2)}, u32[]{:S(2)}) %all-to-all-start.1) | async-done | bytes 4849696 | tf_op jit(solution)/shard_map/all_to_all | solution.py:544
  423.4 4.0 slice_bitcast_fusion
  427.4 2.5 copy.104
  431.3 10.3 %pad_maximum_fusion = bf16[128,10240]{0,1:T(8,128)(2,1)S(1)} fusion(bf16[128,1024]{0,1:T(8,128)(2,1)S(1)} %bitcast.133, bf16[128,1024]{0,1:T(8,128)(2,1)S(1)} %bitcast.132, bf16[128,8192]{0,1:T(8,128)(2,1)} %bitcast.119), kind=kLoop, calls=%fused_computation.3 | loop fusion | flops 7864320 | bytes 5242880 | tf_op jit(solution)/shard_map/concatenate | solution.py:549
  441.6 2.6 copy.111
  444.2 3.0 copy.107
  447.2 2.9 copy.112
  452.2 93.5 %reduce-scatter.2.cloned.1.call-done = f32[1,8,256,128]{3,2,1,0:T(8,128)} async-done(((f32[8,8,256,128]{3,2,1,0:T(8,128)}), f32[1,8,256,128]{3,2,1,0:T(8,128)}) %reduce-scatter.2.cloned.1.call-update) | async-done | bytes 1048592 | tf_op jit(solution)/shard_map/reduce_scatter | solution.py:541
  (141 shorter events, 35.6 us)
Async XLA Ops:
  7.2 132.7 %all-reduce.12.cloned.1.call-start = ((), (), s32[]{:S(2)}) async-start(), calls=%async_computation.6 | async-start | bytes 483328
  11.4 0.7 copy-start.1
  12.1 149.8 %all-gather.4.cloned.1.call-start = ((), (), s32[]{:S(2)}) async-start(), calls=%async_computation.3 | async-start | bytes 4718592 | tf_op jit(solution)/shard_map/all_gather | solution.py:490
  14.2 1.7 copy-start
  16.0 1.6 slice-start
  35.0 4.1 copy-start.6
  50.6 5.6 %copy-start.5 = (s32[128]{0:T(128)S(1)}, s32[128]{0:T(128)}, u32[]{:S(2)}) copy-start(s32[128]{0:T(128)} %param.20) | copy-start | bytes 1540
  50.6 7.0 %copy-start.3 = (bf16[8,3,320]{2,0,1:T(8,128)(2,1)S(1)}, bf16[8,3,320]{2,0,1:T(8,128)(2,1)}, u32[]{:S(2)}) copy-start(bf16[8,3,320]{2,0,1:T(8,128)(2,1)} %param.19) | copy-start | bytes 46084
  50.6 92.4 %all-to-all-start = ((bf16[4,128,6784]{2,1,0:T(8,128)(2,1)}), bf16[4,128,6784]{2,1,0:T(8,128)(2,1)}, u32[]{:S(2)}, u32[]{:S(2)}) async-start(bf16[4,128,6784]{2,1,0:T(8,128)(2,1)} %concatenate.24), calls=%async_computation | async-start | bytes 13893632 | tf_op jit(solution)/shard_map/all_to_all | solution.py:488
  56.1 301.4 %all-reduce.14.cloned.1.call-start = ((), (), s32[]{:S(2)}) async-start(), calls=%async_computation.7 | async-start | bytes 2449408
  134.9 2.7 copy-start.7
  269.4 3.1 copy-start.4
  273.6 1.2 copy-start.2
  276.9 115.3 %all-reduce.10.cloned.1.call-start = ((), (), s32[]{:S(2)}) async-start(), calls=%async_computation.5 | async-start | bytes 311296 | tf_op jit(solution)/shard_map/psum | solution.py:582
  360.6 185.2 %reduce-scatter.2.cloned.1.call-start = ((), (), s32[]{:S(2)}) async-start(), calls=%async_computation.4 | async-start | bytes 9437184 | tf_op jit(solution)/shard_map/reduce_scatter | solution.py:541
  361.2 62.3 %all-to-all-start.1 = ((bf16[4,128,4736]{2,1,0:T(8,128)(2,1)}), bf16[4,128,4736]{2,1,0:T(8,128)(2,1)}, u32[]{:S(2)}, u32[]{:S(2)}) async-start(bf16[4,128,4736]{2,1,0:T(8,128)(2,1)} %get-tuple-element.15), calls=%async_computation.1 | async-start | bytes 9699328 | tf_op jit(solution)/shard_map/all_to_all | solution.py:544
Sparse Core Ops, SparseCore 0:
  12.2 73.1 all-reduce.11
  87.8 74.1 all-gather.3
  277.0 80.4 all-reduce.13
  360.7 31.4 all-reduce.9
  396.2 149.4 reduce-scatter.1

commit v2 on v1

--- a/solution.py
+++ b/solution.py
@@ -430,6 +430,94 @@
     )(prompts, adv, recv, tails, wv, hv, states)
 
 
+def pack_kernel(dims, xp, bp, cp, zp, upp, dtp, lenp, out):
+    inner, gn, heads, docs = dims
+    rows = xp.shape[0]
+    i = pl.program_id(0)
+    at = 0
+    for ref in (xp, bp, cp, zp, upp):
+        width = ref.shape[1]
+        out[0, :, at : at + width] = ref[...]
+        at += width
+    lane = lax.broadcasted_iota(jnp.int32, (1, dtp.shape[1]), 1) // heads
+    own = jnp.where(lane == i, dtp[...], 0.0)
+    dt = sum(own[:, j * heads : (j + 1) * heads] for j in range(dtp.shape[1] // heads))
+    lens = jnp.broadcast_to(lenp[...].astype(F32), (rows, docs)).astype(BF16)
+    pad = jnp.zeros((rows, 128 - 3 * heads - docs), BF16)
+    out[0, :, at:] = jnp.concatenate(list(split3(dt)) + [lens, pad], axis=1)
+
+
+def pack(xbc, zgate, upstream, dt_raw, resp_lengths, dp_count):
+    rows = xbc.shape[0]
+    docs = resp_lengths.shape[1]
+    inner, gn, heads = DI // dp_count, GN // dp_count, H // dp_count
+    width = 3 * inner + 2 * gn + 128
+    return pl.pallas_call(
+        functools.partial(pack_kernel, (inner, gn, heads, docs)),
+        grid=(dp_count,),
+        in_specs=[
+            pl.BlockSpec((rows, inner), lambda i: (0, i)),
+            pl.BlockSpec((rows, gn), lambda i: (0, DI // gn + i)),
+            pl.BlockSpec((rows, gn), lambda i: (0, (DI + GN) // gn + i)),
+            pl.BlockSpec((rows, inner), lambda i: (0, i)),
+            pl.BlockSpec((rows, inner), lambda i: (0, i)),
+            pl.BlockSpec(dt_raw.shape, lambda i: (0, 0)),
+            pl.BlockSpec(resp_lengths.shape, lambda i: (0, 0)),
+        ],
+        out_specs=pl.BlockSpec((1, rows, width), lambda i: (i, 0, 0)),
+        out_shape=jax.ShapeDtypeStruct((dp_count, rows, width), BF16),
+        compiler_params=pltpu.CompilerParams(
+            dimension_semantics=("arbitrary",), vmem_limit_bytes=32 * 1024 * 1024
+        ),
+        name="pack",
+    )(xbc, xbc, xbc, zgate, upstream, dt_raw, resp_lengths)
+
+
+def unpack_kernel(dims, back, gx, gz, gdt):
+    inner, gn, heads = dims
+    i = pl.program_id(0)
+    gx[:, pl.ds(pl.multiple_of(i * inner, inner), inner)] = back[0, :, 0:inner]
+    gx[:, pl.ds(pl.multiple_of(DI + i * gn, gn), gn)] = back[0, :, inner : inner + gn]
+    gx[:, pl.ds(pl.multiple_of(DI + GN + i * gn, gn), gn)] = back[
+        0, :, inner + gn : inner + 2 * gn
+    ]
+    gz[...] = back[0, :, inner + 2 * gn : 2 * inner + 2 * gn]
+    meta = back[0, :, 2 * inner + 2 * gn :].astype(F32)
+    dt = meta[:, 0:heads] + meta[:, heads : 2 * heads] + meta[:, 2 * heads : 3 * heads]
+    wide = jnp.concatenate([dt] * (H // heads), axis=1)
+    lane = lax.broadcasted_iota(jnp.int32, (1, H), 1) // heads
+    gdt[...] = jnp.where(lane == i, wide, gdt[...])
+
+
+def unpack(back):
+    dp_count, rows, width = back.shape
+    inner, gn, heads = DI // dp_count, GN // dp_count, H // dp_count
+    return pl.pallas_call(
+        functools.partial(unpack_kernel, (inner, gn, heads)),
+        grid=(dp_count,),
+        in_specs=[pl.BlockSpec((1, rows, width), lambda i: (i, 0, 0))],
+        out_specs=[
+            pl.BlockSpec((rows, DI + 2 * GN), lambda i: (0, 0)),
+            pl.BlockSpec((rows, inner), lambda i: (0, i)),
+            pl.BlockSpec((rows, H), lambda i: (0, 0)),
+        ],
+        out_shape=[
+            jax.ShapeDtypeStruct((rows, DI + 2 * GN), BF16),
+            jax.ShapeDtypeStruct((rows, DI), BF16),
+            jax.ShapeDtypeStruct((rows, H), F32),
+        ],
+        compiler_params=pltpu.CompilerParams(
+            dimension_semantics=("arbitrary",), vmem_limit_bytes=32 * 1024 * 1024
+        ),
+        name="unpack",
+    )(back)
+
+
+def to_all(a, axes, count):
+    many = jnp.broadcast_to(a[None], (count,) + a.shape)
+    return lax.all_to_all(many, axes, split_axis=0, concat_axis=0, tiled=True)
+
+
 def shards(
     xbc,
     zgate,
@@ -460,31 +548,7 @@
     chans = inner + 2 * gn
     heads = H // dp_count
 
-    def by_dest(a):
-        return a.reshape(rows, dp_count, -1).transpose(1, 0, 2)
-
-    hi = lax.reduce_precision(dt_raw, 8, 7)
-    rest = dt_raw - hi
-    mid = lax.reduce_precision(rest, 8, 7)
-    low = rest - mid
-    lens_cols = jnp.broadcast_to(
-        resp_lengths.astype(BF16).reshape(1, 1, docs), (dp_count, rows, docs)
-    )
-    sent = jnp.concatenate(
-        [
-            by_dest(xbc[:, :DI]),
-            by_dest(xbc[:, DI : DI + GN]),
-            by_dest(xbc[:, DI + GN :]),
-            by_dest(zgate),
-            by_dest(upstream),
-            by_dest(hi.astype(BF16)),
-            by_dest(mid.astype(BF16)),
-            by_dest(low.astype(BF16)),
-            lens_cols,
-            jnp.zeros((dp_count, rows, 128 - 3 * heads - docs), BF16),
-        ],
-        axis=2,
-    )
+    sent = pack(xbc, zgate, upstream, dt_raw, resp_lengths, dp_count)
     recv = lax.all_to_all(sent, "dp", split_axis=0, concat_axis=0, tiled=True)
 
     states = lax.all_gather(
@@ -495,7 +559,7 @@
     flat = jnp.concatenate(
         [conv_weight.reshape(-1), conv_bias, norm_gain, dt_bias, a_log, d_skip]
     )
-    flat = lax.all_gather(flat, "fsdp", axis=0)
+    flat = to_all(flat, "fsdp", fsdp_count)
     conv_all = flat[:, : 5 * chan_w].reshape(fsdp_count, 5, chan_w).transpose(1, 0, 2)
     conv_all = conv_all.reshape(5, fsdp_count * chan_w)
     gain_w = norm_gain.shape[0]
@@ -531,7 +595,7 @@
     adv = advantages(rewards, resp_prompt, prompt_count)
     adv = adv.reshape(-1, docs)[holders].reshape(-1)
 
-    tails = lax.all_gather(conv_tails, ("dp", "fsdp"), axis=0)
+    tails = to_all(conv_tails, ("dp", "fsdp"), dp_count * fsdp_count)
     tails = tails.transpose(1, 2, 0, 3).reshape(prompt_count, 3, -1)
     tails = jnp.pad(own_channels(tails), ((0, 0), (0, 1), (0, 0)))
     tails = tails[prompts].reshape(dp_count, docs * 4, chans)
@@ -543,13 +607,7 @@
 
     back = lax.all_to_all(out, "dp", split_axis=0, concat_axis=0, tiled=True)
 
-    def home(lo, width):
-        return back[:, :, lo : lo + width].transpose(1, 0, 2).reshape(rows, dp_count * width)
-
-    grad_x = jnp.concatenate([home(0, inner), home(inner, gn), home(inner + gn, gn)], axis=1)
-    grad_z = home(chans, inner)
-    parts = [home(chans + inner + i * heads, heads).astype(F32) for i in range(3)]
-    grad_dt = parts[0] + parts[1] + parts[2]
+    grad_x, grad_z, grad_dt = unpack(back)
 
     onehot = (jnp.arange(prompt_count, dtype=jnp.int32)[:, None] == prompts[None, :]).astype(F32)
     dtail = dtail.reshape(dp_count * docs, 4, chans)[:, :3].reshape(dp_count * docs, 3 * chans)
@@ -579,11 +637,19 @@
         ],
         axis=1,
     )
-    summed = lax.psum(lax.psum_scatter(payload, "fsdp", scatter_dimension=0, tiled=False), "dp")
+    summed = jnp.sum(lax.all_to_all(payload, "fsdp", split_axis=0, concat_axis=0, tiled=True), axis=0)
     tail_size = prompt_count * 3 * chan_share
-    grad_tails = lax.dynamic_slice_in_dim(summed, dp_at * tail_size, tail_size)
-    grad_tails = grad_tails.reshape(prompt_count, 3, chan_share)
-    rest = summed[dp_count * tail_size :]
+    shared = summed[dp_count * tail_size :]
+    pieces = jnp.concatenate(
+        [
+            summed[: dp_count * tail_size].reshape(dp_count, tail_size),
+            jnp.broadcast_to(shared[None], (dp_count,) + shared.shape),
+        ],
+        axis=1,
+    )
+    summed = jnp.sum(lax.all_to_all(pieces, "dp", split_axis=0, concat_axis=0, tiled=True), axis=0)
+    grad_tails = summed[:tail_size].reshape(prompt_count, 3, chan_share)
+    rest = summed[tail_size:]
     grad_conv = rest[: 5 * chan_w].reshape(5, chan_w)
     rest = rest[5 * chan_w :]
     per = dt_bias.shape[0]

time: 554 us -> 427 us (0.77)
  waiting for transfers between devices: 244 us -> 166 us
  local copies, waits for them, and re-layouts: 82.2 us -> 24.8 us
  other arithmetic: 13.6 us -> 2.21 us
  blocking collectives: 77.3 us -> 86.9 us
  Pallas kernels: 107 us -> 114 us
    all_to_all x0 -> x3, blocking collectives: none -> 86.9 us  [the longest x1 62.7 us: shards(): lax.all_to_all(payload, 'fsdp', split_axis=0, concat_axis=0, tiled=True)]
    unnamed x7 -> x2, waiting for transfers between devices: 81.9 us -> 0.69 us
    all_gather x1 -> x0, blocking collectives: 77.3 us -> none  [shards(): tails = lax.all_gather(conv_tails, ('dp', 'fsdp'), axis=0)]
    all_to_all x1, waiting for transfers between devices: 0.01 us -> 69.2 us  [shards(): recv = lax.all_to_all(sent, 'dp', split_axis=0, concat_axis=0, tiled=True)]
    reduce_scatter x1, waiting for transfers between devices: 93.5 us -> 27.4 us  [shards(): lax.psum_scatter(dstate, 'fsdp', scatter_dimension=0, tiled=False)]
    all_to_all x1, waiting for transfers between devices: 24.3 us -> 51.9 us  [shards(): back = lax.all_to_all(out, 'dp', split_axis=0, concat_axis=0, tiled=True)]
    psum x1 -> x0, waiting for transfers between devices: 25.7 us -> none  [shards(): lax.psum(lax.psum_scatter(payload, 'fsdp', scatter_dimension=0, tiled=Fal...]
    all_gather x1, waiting for transfers between devices: 19 us -> 0.01 us  [shards(): lax.all_gather(prompt_states.reshape(prompt_count, head_share * P_SIZE, N...]
  transfers between devices with their start and end apart: 7 -> 5, of which waited for: 5 -> 4; matrix products, arithmetic and copies ran while one was open for 14% -> 5% of each run, Pallas kernels for 0% -> 2%
where the time goes in v2:
time: 427 us; the launch traced here: 426 us
  waiting for transfers between devices  166 us (39%)
  Pallas kernels  114 us (27%)
  blocking collectives  86.9 us (20%)
  local copies, waits for them, and re-layouts  24.8 us (6%)
  starting transfers between devices  15.7 us (4%)
  between operations  14.6 us (3%)
    pallas_call x1, Pallas kernels, run_mixer(): pl.pallas_call(functools.partial(mixer_kernel, dims), grid=(blocks,), in_...  108 us
    all_to_all x1, waiting for transfers between devices, shards(): recv = lax.all_to_all(sent, 'dp', split_axis=0, concat_axis=0, tiled=True)  69.2 us
    all_to_all x1, blocking collectives, shards(): lax.all_to_all(payload, 'fsdp', split_axis=0, concat_axis=0, tiled=True)  62.7 us
    all_to_all x1, waiting for transfers between devices, shards(): back = lax.all_to_all(out, 'dp', split_axis=0, concat_axis=0, tiled=True)  51.9 us
    reduce_scatter x1, waiting for transfers between devices, shards(): lax.psum_scatter(dstate, 'fsdp', scatter_dimension=0, tiled=False)  27.4 us
    all_to_all x1, waiting for transfers between devices, to_all(): return lax.all_to_all(many, axes, split_axis=0, concat_axis=0, tiled=True)  17.1 us
    all_to_all x1, blocking collectives, to_all(): return lax.all_to_all(many, axes, split_axis=0, concat_axis=0, tiled=True)  16 us
    unnamed x31, local copies, waits for them, and re-layouts  8.9 us
  transfers between devices with their start and end apart: 5, of which 4 were waited for; matrix products, arithmetic and copies ran while one was open for 5% of the time, Pallas kernels for 2%

profile of v2, /device:TPU:0, one launch (start us, length us, event | category | flops | bytes accessed | tf_op | source)
XLA Modules:
  0.0 426.2 jit_solution(4062979311070386978)
XLA Ops:
  7.9 0.9 reshape.173
  8.8 0.8 concatenate.22
  9.8 16.0 %all_to_all.42 = f32[8,1,7472]{2,1,0:T(1,128)S(1)} all-to-all(f32[8,1,7472]{2,1,0:T(1,128)S(1)} %broadcast_in_dim.23), channel_id=1, replica_groups=mesh['dp'=4,'fsdp'=8] {'fsdp'}, dimensions={0} | all-to-all | bytes 478208 | tf_op jit(solution)/shard_map/all_to_all | solution.py:518
  25.7 0.9 broadcast_in_dim.22
  26.6 5.2 %all-to-all-start.1 = ((bf16[32,8,3,320]{3,1,2,0:T(8,128)(2,1)}), bf16[32,8,3,320]{3,1,2,0:T(8,128)(2,1)S(1)}, u32[]{:S(2)}, u32[]{:S(2)}) async-start(bf16[32,8,3,320]{3,1,2,0:T(8,128)(2,1)} %broadcast_in_dim.22), calls=%async_computation.1 | async-start | bytes 1179648 | tf_op jit(solution)/shard_map/all_to_all | solution.py:518
  31.8 1.6 copy-done.2
  33.4 1.6 copy-done.3
  35.0 1.5 pack.1
  36.5 2.9 copy-done
  39.4 17.1 %all-to-all-done.1 = bf16[32,8,3,320]{3,1,2,0:T(8,128)(2,1)S(1)} async-done(((bf16[32,8,3,320]{3,1,2,0:T(8,128)(2,1)}), bf16[32,8,3,320]{3,1,2,0:T(8,128)(2,1)S(1)}, u32[]{:S(2)}, u32[]{:S(2)}) %all-to-all-start.1) | async-done | bytes 491552 | tf_op jit(solution)/shard_map/all_to_all | solution.py:518
  56.5 5.4 %all-to-all-start = ((bf16[4,128,6784]{2,1,0:T(8,128)(2,1)}), bf16[4,128,6784]{2,1,0:T(8,128)(2,1)}, u32[]{:S(2)}, u32[]{:S(2)}) async-start(bf16[4,128,6784]{2,1,0:T(8,128)(2,1)} %copy-done), calls=%async_computation | async-start | bytes 13893632 | tf_op jit(solution)/shard_map/all_to_all | solution.py:552
  68.6 0.8 gather_fusion.2
  69.6 0.8 reshape.172.tails_ref
  70.4 69.2 %all-to-all-done.recv_ref = bf16[4,128,6784]{2,1,0:T(8,128)(2,1)} async-done(((bf16[4,128,6784]{2,1,0:T(8,128)(2,1)}), bf16[4,128,6784]{2,1,0:T(8,128)(2,1)}, u32[]{:S(2)}, u32[]{:S(2)}) %all-to-all-start) | async-done | bytes 6946848 | tf_op jit(solution)/shard_map/all_to_all | solution.py:552
  139.7 107.5 %mixer.1 = (bf16[4,128,4736]{2,1,0:T(8,128)(2,1)}, f32[8,8,256,128]{3,2,1,0:T(8,128)}, f32[4,16,2560]{2,1,0:T(8,128)}, f32[16,2560]{1,0:T(8,128)}) custom-call(s32[16]{0:T(128)} %reshape.167.prompt_ref, f32[16]{0:T(128)} %reshape.169.adv_ref, bf16[4,128,6784]{2,1,0:T(8,128)(2,1)} %all-to-all-done.recv_ref, bf16[4,16,2560]{2,1,0:T(8,128)(2,1)} %reshape.172.tails_ref, ...), custom_call_target="tpu_custom_call" | custom-call | flops 20000000000 | bytes 30000000 | tf_op jit(solution)/shard_map/mixer/pallas_call | solution.py:379
  247.2 1.1 copy-done.6
  252.8 1.3 copy.44
  254.0 62.7 %all_to_all.43 = f32[8,1,38192]{2,1,0:T(1,128)S(1)} all-to-all(f32[8,1,38192]{2,1,0:T(1,128)S(1)} %copy.44), channel_id=1, replica_groups=mesh['dp'=4,'fsdp'=8] {'fsdp'}, dimensions={0} | all-to-all | bytes 2444288 | tf_op jit(solution)/shard_map/all_to_all | solution.py:640
  316.8 0.9 reduce_sum.28
  318.0 8.2 %all_to_all.44 = f32[4,1,15152]{2,1,0:T(1,128)S(1)} all-to-all(f32[4,1,15152]{2,1,0:T(1,128)S(1)} %all_to_all.34), channel_id=1, replica_groups=mesh['dp'=4,'fsdp'=8] {'dp'}, dimensions={0} | all-to-all | bytes 484864 | tf_op jit(solution)/shard_map/all_to_all | solution.py:650
  326.2 5.1 %all-to-all-start.3 = ((bf16[4,128,4736]{2,1,0:T(8,128)(2,1)}), bf16[4,128,4736]{2,1,0:T(8,128)(2,1)}, u32[]{:S(2)}, u32[]{:S(2)}) async-start(bf16[4,128,4736]{2,1,0:T(8,128)(2,1)} %get-tuple-element.18), calls=%async_computation.3 | async-start | bytes 9699328 | tf_op jit(solution)/shard_map/all_to_all | solution.py:608
  334.7 51.9 %all-to-all-done.3.back = bf16[4,128,4736]{2,1,0:T(8,128)(2,1)} async-done(((bf16[4,128,4736]{2,1,0:T(8,128)(2,1)}), bf16[4,128,4736]{2,1,0:T(8,128)(2,1)}, u32[]{:S(2)}, u32[]{:S(2)}) %all-to-all-start.3) | async-done | bytes 4849696 | tf_op jit(solution)/shard_map/all_to_all | solution.py:608
  386.6 5.4 %unpack.1 = (bf16[128,10240]{1,0:T(8,128)(2,1)}, bf16[128,8192]{1,0:T(8,128)(2,1)}, f32[128,128]{1,0:T(8,128)}) custom-call(bf16[4,128,4736]{2,1,0:T(8,128)(2,1)} %all-to-all-done.3.back), custom_call_target="tpu_custom_call" | custom-call | tf_op jit(solution)/shard_map/unpack/pallas_call | solution.py:495
  392.0 27.4 %reduce-scatter.2.cloned.1.call-done = f32[1,8,256,128]{3,2,1,0:T(8,128)} async-done(((f32[8,8,256,128]{3,2,1,0:T(8,128)}), f32[1,8,256,128]{3,2,1,0:T(8,128)}) %reduce-scatter.2.cloned.1.call-update) | async-done | bytes 1048592 | tf_op jit(solution)/shard_map/reduce_scatter | solution.py:605
  (116 shorter events, 15.6 us)
Async XLA Ops:
  7.2 18.5 %copy-start.8 = (bf16[8,3,320]{2,0,1:T(8,128)(2,1)S(1)}, bf16[8,3,320]{2,0,1:T(8,128)(2,1)}, u32[]{:S(2)}) copy-start(bf16[8,3,320]{2,0,1:T(8,128)(2,1)} %param.19) | copy-start | bytes 46084
  7.2 132.5 %all-gather.2.cloned.1.call-start = ((), (), s32[]{:S(2)}) async-start(), calls=%async_computation.7 | async-start | bytes 4718592 | tf_op jit(solution)/shard_map/all_gather | solution.py:554
  7.2 24.5 %copy-start.4 = (f32[128,128]{1,0:T(8,128)S(1)}, f32[128,128]{1,0:T(8,128)}, u32[]{:S(2)}) copy-start(f32[128,128]{1,0:T(8,128)} %dtp.1) | copy-start | bytes 196612
  7.9 23.8 %copy-start.1 = (bf16[128,10240]{1,0:T(8,128)(2,1)S(1)}, bf16[128,10240]{1,0:T(8,128)(2,1)}, u32[]{:S(2)}) copy-start(bf16[128,10240]{1,0:T(8,128)(2,1)} %cp.1) | copy-start | bytes 7864324
  9.6 22.2 %copy-start.5 = (s32[1,4]{1,0:T(1,128)S(1)}, s32[1,4]{1,0:T(1,128)}, u32[]{:S(2)}) copy-start(s32[1,4]{1,0:T(1,128)} %lenp.1) | copy-start | bytes 52
  26.6 29.9 %all-to-all-start.1 = ((bf16[32,8,3,320]{3,1,2,0:T(8,128)(2,1)}), bf16[32,8,3,320]{3,1,2,0:T(8,128)(2,1)S(1)}, u32[]{:S(2)}, u32[]{:S(2)}) async-start(bf16[32,8,3,320]{3,1,2,0:T(8,128)(2,1)} %broadcast_in_dim.22), calls=%async_computation.1 | async-start | bytes 1179648 | tf_op jit(solution)/shard_map/all_to_all | solution.py:518
  31.8 1.6 copy-start.2
  33.4 1.6 copy-start.3
  36.5 2.9 copy-start
  39.4 22.6 %copy-start.10 = (s32[128]{0:T(128)S(1)}, s32[128]{0:T(128)}, u32[]{:S(2)}) copy-start(s32[128]{0:T(128)} %param.20) | copy-start | bytes 1540
  39.4 24.0 %copy-start.11 = (f32[128]{0:T(128)S(1)}, f32[128]{0:T(128)}, u32[]{:S(2)}) copy-start(f32[128]{0:T(128)} %param.22) | copy-start | bytes 1540
  56.5 83.1 %all-to-all-start = ((bf16[4,128,6784]{2,1,0:T(8,128)(2,1)}), bf16[4,128,6784]{2,1,0:T(8,128)(2,1)}, u32[]{:S(2)}, u32[]{:S(2)}) async-start(bf16[4,128,6784]{2,1,0:T(8,128)(2,1)} %copy-done), calls=%async_computation | async-start | bytes 13893632 | tf_op jit(solution)/shard_map/all_to_all | solution.py:552
  61.9 357.5 %reduce-scatter.2.cloned.1.call-start = ((), (), s32[]{:S(2)}) async-start(), calls=%async_computation.8 | async-start | bytes 9437184 | tf_op jit(solution)/shard_map/reduce_scatter | solution.py:605
  247.2 1.1 copy-start.6
  248.3 0.7 copy-start.9
  250.7 1.0 copy-start.7
  326.2 60.3 %all-to-all-start.3 = ((bf16[4,128,4736]{2,1,0:T(8,128)(2,1)}), bf16[4,128,4736]{2,1,0:T(8,128)(2,1)}, u32[]{:S(2)}, u32[]{:S(2)}) async-start(bf16[4,128,4736]{2,1,0:T(8,128)(2,1)} %get-tuple-element.18), calls=%async_computation.3 | async-start | bytes 9699328 | tf_op jit(solution)/shard_map/all_to_all | solution.py:608
Sparse Core Ops, SparseCore 0:
  10.1 86.4 all-gather.1
  247.3 172.0 reduce-scatter.1

commit v3 on v2

--- a/solution.py
+++ b/solution.py
@@ -430,10 +430,10 @@
     )(prompts, adv, recv, tails, wv, hv, states)
 
 
-def pack_kernel(dims, xp, bp, cp, zp, upp, dtp, lenp, out):
+def pack_kernel(dims, me, xp, bp, cp, zp, upp, dtp, lenp, out):
     inner, gn, heads, docs = dims
     rows = xp.shape[0]
-    i = pl.program_id(0)
+    i = me[0] ^ pl.program_id(0)
     at = 0
     for ref in (xp, bp, cp, zp, upp):
         width = ref.shape[1]
@@ -447,35 +447,38 @@
     out[0, :, at:] = jnp.concatenate(list(split3(dt)) + [lens, pad], axis=1)
 
 
-def pack(xbc, zgate, upstream, dt_raw, resp_lengths, dp_count):
+def pack(me, xbc, zgate, upstream, dt_raw, resp_lengths, dp_count):
     rows = xbc.shape[0]
     docs = resp_lengths.shape[1]
     inner, gn, heads = DI // dp_count, GN // dp_count, H // dp_count
     width = 3 * inner + 2 * gn + 128
     return pl.pallas_call(
         functools.partial(pack_kernel, (inner, gn, heads, docs)),
-        grid=(dp_count,),
-        in_specs=[
-            pl.BlockSpec((rows, inner), lambda i: (0, i)),
-            pl.BlockSpec((rows, gn), lambda i: (0, DI // gn + i)),
-            pl.BlockSpec((rows, gn), lambda i: (0, (DI + GN) // gn + i)),
-            pl.BlockSpec((rows, inner), lambda i: (0, i)),
-            pl.BlockSpec((rows, inner), lambda i: (0, i)),
-            pl.BlockSpec(dt_raw.shape, lambda i: (0, 0)),
-            pl.BlockSpec(resp_lengths.shape, lambda i: (0, 0)),
-        ],
-        out_specs=pl.BlockSpec((1, rows, width), lambda i: (i, 0, 0)),
+        grid_spec=pltpu.PrefetchScalarGridSpec(
+            num_scalar_prefetch=1,
+            grid=(dp_count,),
+            in_specs=[
+                pl.BlockSpec((rows, inner), lambda o, me: (0, o ^ me[0])),
+                pl.BlockSpec((rows, gn), lambda o, me: (0, DI // gn + (o ^ me[0]))),
+                pl.BlockSpec((rows, gn), lambda o, me: (0, (DI + GN) // gn + (o ^ me[0]))),
+                pl.BlockSpec((rows, inner), lambda o, me: (0, o ^ me[0])),
+                pl.BlockSpec((rows, inner), lambda o, me: (0, o ^ me[0])),
+                pl.BlockSpec(dt_raw.shape, lambda o, me: (0, 0)),
+                pl.BlockSpec(resp_lengths.shape, lambda o, me: (0, 0)),
+            ],
+            out_specs=pl.BlockSpec((1, rows, width), lambda o, me: (o, 0, 0)),
+        ),
         out_shape=jax.ShapeDtypeStruct((dp_count, rows, width), BF16),
         compiler_params=pltpu.CompilerParams(
             dimension_semantics=("arbitrary",), vmem_limit_bytes=32 * 1024 * 1024
         ),
         name="pack",
-    )(xbc, xbc, xbc, zgate, upstream, dt_raw, resp_lengths)
-
-
-def unpack_kernel(dims, back, gx, gz, gdt):
+    )(me, xbc, xbc, xbc, zgate, upstream, dt_raw, resp_lengths)
+
+
+def unpack_kernel(dims, me, back, gx, gz, gdt):
     inner, gn, heads = dims
-    i = pl.program_id(0)
+    i = me[0] ^ pl.program_id(0)
     gx[:, pl.ds(pl.multiple_of(i * inner, inner), inner)] = back[0, :, 0:inner]
     gx[:, pl.ds(pl.multiple_of(DI + i * gn, gn), gn)] = back[0, :, inner : inner + gn]
     gx[:, pl.ds(pl.multiple_of(DI + GN + i * gn, gn), gn)] = back[
@@ -489,18 +492,21 @@
     gdt[...] = jnp.where(lane == i, wide, gdt[...])
 
 
-def unpack(back):
+def unpack(me, back):
     dp_count, rows, width = back.shape
     inner, gn, heads = DI // dp_count, GN // dp_count, H // dp_count
     return pl.pallas_call(
         functools.partial(unpack_kernel, (inner, gn, heads)),
-        grid=(dp_count,),
-        in_specs=[pl.BlockSpec((1, rows, width), lambda i: (i, 0, 0))],
-        out_specs=[
-            pl.BlockSpec((rows, DI + 2 * GN), lambda i: (0, 0)),
-            pl.BlockSpec((rows, inner), lambda i: (0, i)),
-            pl.BlockSpec((rows, H), lambda i: (0, 0)),
-        ],
+        grid_spec=pltpu.PrefetchScalarGridSpec(
+            num_scalar_prefetch=1,
+            grid=(dp_count,),
+            in_specs=[pl.BlockSpec((1, rows, width), lambda o, me: (o, 0, 0))],
+            out_specs=[
+                pl.BlockSpec((rows, DI + 2 * GN), lambda o, me: (0, 0)),
+                pl.BlockSpec((rows, inner), lambda o, me: (0, o ^ me[0])),
+                pl.BlockSpec((rows, H), lambda o, me: (0, 0)),
+            ],
+        ),
         out_shape=[
             jax.ShapeDtypeStruct((rows, DI + 2 * GN), BF16),
             jax.ShapeDtypeStruct((rows, DI), BF16),
@@ -510,7 +516,34 @@
             dimension_semantics=("arbitrary",), vmem_limit_bytes=32 * 1024 * 1024
         ),
         name="unpack",
-    )(back)
+    )(me, back)
+
+
+def swap_blocks(blocks, count):
+    got = [blocks[0]]
+    for o in range(1, count):
+        got.append(lax.ppermute(blocks[o], "dp", [(i, i ^ o) for i in range(count)]))
+    return jnp.stack(got)
+
+
+def ring_sums(table, at, count):
+    ring = list(range(0, count, 2)) + list(range(1, count, 2))[::-1]
+    place = [ring.index(j) for j in range(count)]
+    ring_at = jnp.asarray(ring, jnp.int32)
+    here = jnp.asarray(place, jnp.int32)[at]
+    half = table.shape[1] // 2
+
+    def part(way, steps):
+        owner = ring_at[(here - way * (1 + steps)) % count]
+        start = (owner, 0 if way == 1 else half, 0, 0)
+        return lax.dynamic_slice(table, start, (1, half) + table.shape[2:])[0]
+
+    held = {way: part(way, 0) for way in (1, -1)}
+    for hop in range(1, count):
+        for way in (1, -1):
+            pairs = [(ring[r], ring[(r + way) % count]) for r in range(count)]
+            held[way] = lax.ppermute(held[way], "fsdp", pairs) + part(way, hop)
+    return jnp.concatenate([held[1], held[-1]], axis=0)
 
 
 def to_all(a, axes, count):
@@ -548,8 +581,9 @@
     chans = inner + 2 * gn
     heads = H // dp_count
 
-    sent = pack(xbc, zgate, upstream, dt_raw, resp_lengths, dp_count)
-    recv = lax.all_to_all(sent, "dp", split_axis=0, concat_axis=0, tiled=True)
+    me = dp_at.astype(jnp.int32).reshape(1)
+    sent = pack(me, xbc, zgate, upstream, dt_raw, resp_lengths, dp_count)
+    recv = swap_blocks(sent, dp_count)
 
     states = lax.all_gather(
         prompt_states.reshape(prompt_count, head_share * P_SIZE, N), "fsdp", axis=0
@@ -590,7 +624,7 @@
     )
     hv = jnp.concatenate([per_head[:2], jnp.zeros((6, heads), F32)])
 
-    holders = jnp.arange(dp_count, dtype=jnp.int32) * fsdp_count + fsdp_at
+    holders = (jnp.arange(dp_count, dtype=jnp.int32) ^ dp_at) * fsdp_count + fsdp_at
     prompts = resp_prompt.reshape(-1, docs)[holders].reshape(-1)
     adv = advantages(rewards, resp_prompt, prompt_count)
     adv = adv.reshape(-1, docs)[holders].reshape(-1)
@@ -602,12 +636,12 @@
 
     out, dstate, dtail, wg = run_mixer(prompts, adv, recv, tails, wv, hv, states, docs)
 
-    grad_states = lax.psum_scatter(dstate, "fsdp", scatter_dimension=0, tiled=False)
+    grad_states = ring_sums(dstate, fsdp_at, fsdp_count)
     grad_states = grad_states.reshape(prompt_count, head_share, P_SIZE, N)
 
-    back = lax.all_to_all(out, "dp", split_axis=0, concat_axis=0, tiled=True)
-
-    grad_x, grad_z, grad_dt = unpack(back)
+    back = swap_blocks(out, dp_count)
+
+    grad_x, grad_z, grad_dt = unpack(me, back)
 
     onehot = (jnp.arange(prompt_count, dtype=jnp.int32)[:, None] == prompts[None, :]).astype(F32)
     dtail = dtail.reshape(dp_count * docs, 4, chans)[:, :3].reshape(dp_count * docs, 3 * chans)
@@ -637,7 +671,11 @@
         ],
         axis=1,
     )
-    summed = jnp.sum(lax.all_to_all(payload, "fsdp", split_axis=0, concat_axis=0, tiled=True), axis=0)
+    used = payload.shape[1]
+    lines = -(-used // 1024) * 8
+    payload = jnp.pad(payload, ((0, 0), (0, lines * 128 - used))).reshape(fsdp_count, lines, 128)
+    summed = lax.psum_scatter(payload, "fsdp", scatter_dimension=0, tiled=False)
+    summed = summed.reshape(-1)[:used]
     tail_size = prompt_count * 3 * chan_share
     shared = summed[dp_count * tail_size :]
     pieces = jnp.concatenate(

time: 427 us -> 387 us (0.906)
  blocking collectives: 86.9 us -> 0 us
  waiting for transfers between devices: 166 us -> 111 us
  between operations: 14.6 us -> 55.4 us
  other arithmetic: 2.21 us -> 25.5 us
  starting transfers between devices: 15.7 us -> 37.7 us
  local copies, waits for them, and re-layouts: 24.8 us -> 42.5 us
    all_to_all x2 -> x1, waiting for transfers between devices: 121 us -> 0.01 us  [shards(): lax.all_to_all(pieces, 'dp', split_axis=0, concat_axis=0, tiled=True)]
    all_to_all x3 -> x0, blocking collectives: 86.9 us -> none  [the longest x1 62.7 us: shards(): lax.all_to_all(payload, 'fsdp', split_axis=0, concat_axis=0, tiled=True)]
    ppermute x0 -> x20, waiting for transfers between devices: none -> 31.7 us  [the longest x14 31.7 us: ring_sums(): held[way] = lax.ppermute(held[way], 'fsdp', pairs) + part(way, hop)]
    all_to_all x1 -> x2, waiting for transfers between devices: 17.1 us -> 47.5 us  [to_all(): return lax.all_to_all(many, axes, split_axis=0, concat_axis=0, tiled=True)]
    ppermute x0 -> x20, starting transfers between devices: none -> 20.9 us  [the longest x14 17.2 us: ring_sums(): held[way] = lax.ppermute(held[way], 'fsdp', pairs) + part(way, hop)]
    add x0 -> x7, other arithmetic: none -> 13.5 us  [ring_sums(): held[way] = lax.ppermute(held[way], 'fsdp', pairs) + part(way, hop)]
    another operation x0 -> x2, other arithmetic: none -> 8.38 us  [swap_blocks(): return jnp.stack(got)]
    all_to_all x1 -> x2, starting transfers between devices: 5.15 us -> 13.3 us  [to_all(): return lax.all_to_all(many, axes, split_axis=0, concat_axis=0, tiled=True)]
  transfers between devices with their start and end apart: 5 -> 25, of which waited for: 4 -> 10; matrix products, arithmetic and copies ran while one was open for 5% -> 14% of each run, Pallas kernels for 2% -> 1%
where the time goes in v3:
time: 387 us; the launch traced here: 385 us
  Pallas kernels  112 us (29%)
  waiting for transfers between devices  111 us (29%)
  between operations  55.4 us (14%)
  local copies, waits for them, and re-layouts  42.5 us (11%)
  starting transfers between devices  37.7 us (10%)
  other arithmetic  25.5 us (7%)
    pallas_call x1, Pallas kernels, run_mixer(): pl.pallas_call(functools.partial(mixer_kernel, dims), grid=(blocks,), in_...  108 us
    all_to_all x2, waiting for transfers between devices, to_all(): return lax.all_to_all(many, axes, split_axis=0, concat_axis=0, tiled=True)  47.5 us
    ppermute x14, waiting for transfers between devices, ring_sums(): held[way] = lax.ppermute(held[way], 'fsdp', pairs) + part(way, hop)  31.7 us
    reduce_scatter x1, waiting for transfers between devices, shards(): summed = lax.psum_scatter(payload, 'fsdp', scatter_dimension=0, tiled=False)  30.7 us
    ppermute x14, starting transfers between devices, ring_sums(): held[way] = lax.ppermute(held[way], 'fsdp', pairs) + part(way, hop)  17.2 us
    add x7, other arithmetic, ring_sums(): held[way] = lax.ppermute(held[way], 'fsdp', pairs) + part(way, hop)  13.5 us
    all_to_all x2, starting transfers between devices, to_all(): return lax.all_to_all(many, axes, split_axis=0, concat_axis=0, tiled=True)  13.3 us
    another operation x2, other arithmetic, swap_blocks(): return jnp.stack(got)  8.38 us
  transfers between devices with their start and end apart: 25, of which 10 were waited for; matrix products, arithmetic and copies ran while one was open for 14% of the time, Pallas kernels for 1%

profile of v3, /device:TPU:0, one launch (start us, length us, event | category | flops | bytes accessed | tf_op | source)
XLA Modules:
  0.0 385.0 jit_solution(13882344230953028837)
XLA Ops:
  10.3 7.3 %all-to-all-start.1 = ((f32[8,1,7472]{2,1,0:T(1,128)}), f32[8,1,7472]{2,1,0:T(1,128)S(1)}, u32[]{:S(2)}, u32[]{:S(2)}) async-start(f32[8,1,7472]{2,1,0:T(1,128)} %broadcast_in_dim.23), calls=%async_computation.1 | async-start | bytes 483328 | tf_op jit(solution)/shard_map/all_to_all | solution.py:551
  17.6 1.7 copy-done
  19.3 1.7 copy-done.1
  21.0 1.8 copy-done.2
  26.0 2.5 fusion.20
  58.1 6.0 %all-to-all-start = ((bf16[32,8,3,320]{3,1,2,0:T(8,128)(2,1)}), bf16[32,8,3,320]{3,1,2,0:T(8,128)(2,1)S(1)}, u32[]{:S(2)}, u32[]{:S(2)}) async-start(bf16[32,8,3,320]{3,1,2,0:T(8,128)(2,1)} %broadcast_in_dim.22), calls=%async_computation | async-start | bytes 1179648 | tf_op jit(solution)/shard_map/all_to_all | solution.py:551
  66.1 47.5 %all-to-all-done = bf16[32,8,3,320]{3,1,2,0:T(8,128)(2,1)S(1)} async-done(((bf16[32,8,3,320]{3,1,2,0:T(8,128)(2,1)}), bf16[32,8,3,320]{3,1,2,0:T(8,128)(2,1)S(1)}, u32[]{:S(2)}, u32[]{:S(2)}) %all-to-all-start) | async-done | bytes 491552 | tf_op jit(solution)/shard_map/all_to_all | solution.py:551
  118.9 6.0 %pad_maximum_fusion.recv_ref = bf16[4,128,6784]{2,1,0:T(8,128)(2,1)} fusion(bf16[1,128,6784]{2,1,0:T(8,128)(2,1)} %bitcast.15, bf16[1,128,6784]{2,1,0:T(8,128)(2,1)} %bitcast.13, bf16[1,128,6784]{2,1,0:T(8,128)(2,1)} %bitcast.11, bf16[1,128,6784]{2,1,0:T(8,128)(2,1)S(1)} %get-tuple-element.74), kind=kLoop, calls=%fused_computation.3 | loop fusion | flops 10420224 | bytes 13893632 | tf_op jit(solution)/shard_map/stack | solution.py:526
  124.9 107.5 %mixer.1 = (bf16[4,128,4736]{2,1,0:T(8,128)(2,1)}, f32[8,8,256,128]{3,2,1,0:T(8,128)}, f32[4,16,2560]{2,1,0:T(8,128)}, f32[16,2560]{1,0:T(8,128)}) custom-call(s32[16]{0:T(128)} %reshape.212.prompt_ref, f32[16]{0:T(128)} %reshape.214.adv_ref, bf16[4,128,6784]{2,1,0:T(8,128)(2,1)} %pad_maximum_fusion.recv_ref, bf16[4,16,2560]{2,1,0:T(8,128)(2,1)} %reshape.217.tails_ref, ...), custom_call_target="tpu_custom_call" | custom-call | flops 20000000000 | bytes 30000000 | tf_op jit(solution)/shard_map/mixer/pallas_call | solution.py:379
  237.8 11.7 %collective-permute-done.13 = f32[4,256,128]{2,1,0:T(8,128)S(1)} collective-permute-done((f32[4,256,128]{2,1,0:T(8,128)S(1)}, f32[4,256,128]{2,1,0:T(8,128)S(1)}, u32[]{:S(2)}, u32[]{:S(2)}) %collective-permute-start.13) | collective-permute-done | bytes 524320 | tf_op jit(solution)/shard_map/ppermute | solution.py:545
  250.9 1.7 collective-permute-start.14
  253.0 11.0 %collective-permute-done.14 = f32[4,256,128]{2,1,0:T(8,128)S(1)} collective-permute-done((f32[4,256,128]{2,1,0:T(8,128)S(1)}, f32[4,256,128]{2,1,0:T(8,128)S(1)}, u32[]{:S(2)}, u32[]{:S(2)}) %collective-permute-start.14) | collective-permute-done | bytes 524320 | tf_op jit(solution)/shard_map/ppermute | solution.py:545
  264.7 2.1 bitcast_add_fusion.12
  280.9 2.1 collective-permute-start.16
  298.2 2.1 bitcast_add_fusion.10
  301.8 3.4 collective-permute-start.17
  305.2 4.2 %fusion.21 = (bf16[1,128,4736]{2,1,0:T(8,128)(2,1)S(1)}, bf16[128,4736]{1,0:T(8,128)(2,1)S(1)}, bf16[128,4736]{1,0:T(8,128)(2,1)}, bf16[128,4736]{1,0:T(8,128)(2,1)}) fusion(bf16[4,128,4736]{2,1,0:T(8,128)(2,1)} %get-tuple-element.18), kind=kLoop, calls=%fused_computation.86 | loop fusion | bytes 9699328 | tf_op jit(solution)/shard_map/slice | solution.py:523
  311.2 30.7 %reduce-scatter.2.cloned.1.call-done = f32[1,304,128]{2,1,0:T(8,128)} async-done(((f32[8,304,128]{2,1,0:T(8,128)}), f32[1,304,128]{2,1,0:T(8,128)}) %reduce-scatter.2.cloned.1.call-update) | async-done | bytes 155664 | tf_op jit(solution)/shard_map/reduce_scatter | solution.py:677
  345.9 2.4 bitcast_add_fusion.9
  351.3 3.4 all-to-all-start.2
  354.7 6.0 %collective-permute-done.11 = f32[4,256,128]{2,1,0:T(8,128)S(1)} collective-permute-done((f32[4,256,128]{2,1,0:T(8,128)}, f32[4,256,128]{2,1,0:T(8,128)S(1)}, u32[]{:S(2)}, u32[]{:S(2)}) %collective-permute-start.11) | collective-permute-done | bytes 524320 | tf_op jit(solution)/shard_map/ppermute | solution.py:545
  361.5 2.4 bitcast_add_fusion.8
  365.9 2.4 pad_maximum_fusion.1.back
  368.3 3.0 unpack.1
  (169 shorter events, 59.2 us)
Async XLA Ops:
  7.2 117.7 %all-gather.2.cloned.1.call-start = ((), (), s32[]{:S(2)}) async-start(), calls=%async_computation.4 | async-start | bytes 4718592 | tf_op jit(solution)/shard_map/all_gather | solution.py:588
  10.3 47.0 %all-to-all-start.1 = ((f32[8,1,7472]{2,1,0:T(1,128)}), f32[8,1,7472]{2,1,0:T(1,128)S(1)}, u32[]{:S(2)}, u32[]{:S(2)}) async-start(f32[8,1,7472]{2,1,0:T(1,128)} %broadcast_in_dim.23), calls=%async_computation.1 | async-start | bytes 483328 | tf_op jit(solution)/shard_map/all_to_all | solution.py:551
  28.5 90.4 %collective-permute-start = (bf16[128,6784]{1,0:T(8,128)(2,1)}, bf16[128,6784]{1,0:T(8,128)(2,1)}, u32[]{:S(2)}, u32[]{:S(2)}) collective-permute-start(bf16[128,6784]{1,0:T(8,128)(2,1)} %get-tuple-element.77), channel_id=1, source_target_pairs={{0,8},{8,0},{16,24},{24,16},{1,9},{9,1},{17,25},{25,17},{2,10},{10... | collective-permute-start | bytes 5210120 | tf_op jit(solution)/shard_map/ppermute | solution.py:525
  28.5 90.4 %collective-permute-start.1 = (bf16[128,6784]{1,0:T(8,128)(2,1)}, bf16[128,6784]{1,0:T(8,128)(2,1)}, u32[]{:S(2)}, u32[]{:S(2)}) collective-permute-start(bf16[128,6784]{1,0:T(8,128)(2,1)} %get-tuple-element.76), channel_id=1, source_target_pairs={{0,16},{8,24},{16,0},{24,8},{1,17},{9,25},{17,1},{25,9},{2,18},{10... | collective-permute-start | bytes 5210120 | tf_op jit(solution)/shard_map/ppermute | solution.py:525
  29.9 89.0 %collective-permute-start.2 = (bf16[128,6784]{1,0:T(8,128)(2,1)}, bf16[128,6784]{1,0:T(8,128)(2,1)}, u32[]{:S(2)}, u32[]{:S(2)}) collective-permute-start(bf16[128,6784]{1,0:T(8,128)(2,1)} %get-tuple-element.75), channel_id=1, source_target_pairs={{0,24},{8,16},{16,8},{24,0},{1,25},{9,17},{17,9},{25,1},{2,26},{10... | collective-permute-start | bytes 5210120 | tf_op jit(solution)/shard_map/ppermute | solution.py:525
  58.1 55.5 %all-to-all-start = ((bf16[32,8,3,320]{3,1,2,0:T(8,128)(2,1)}), bf16[32,8,3,320]{3,1,2,0:T(8,128)(2,1)S(1)}, u32[]{:S(2)}, u32[]{:S(2)}) async-start(bf16[32,8,3,320]{3,1,2,0:T(8,128)(2,1)} %broadcast_in_dim.22), calls=%async_computation | async-start | bytes 1179648 | tf_op jit(solution)/shard_map/all_to_all | solution.py:551
  64.1 277.8 %reduce-scatter.2.cloned.1.call-start = ((), (), s32[]{:S(2)}) async-start(), calls=%async_computation.5 | async-start | bytes 1400832 | tf_op jit(solution)/shard_map/reduce_scatter | solution.py:677
  235.5 14.0 %collective-permute-start.13 = (f32[4,256,128]{2,1,0:T(8,128)S(1)}, f32[4,256,128]{2,1,0:T(8,128)S(1)}, u32[]{:S(2)}, u32[]{:S(2)}) collective-permute-start(f32[4,256,128]{2,1,0:T(8,128)S(1)} %get-tuple-element.73), channel_id=1, source_target_pairs={{0,1},{2,0},{4,2},{6,4},{7,6},{5,7},{3,5},{1,3},{8,9},{10,8},{12,1... | collective-permute-start | bytes 1572872 | tf_op jit(solution)/shard_map/ppermute | solution.py:545
  236.6 13.0 %collective-permute-start.6 = (f32[4,256,128]{2,1,0:T(8,128)S(1)}, f32[4,256,128]{2,1,0:T(8,128)S(1)}, u32[]{:S(2)}, u32[]{:S(2)}) collective-permute-start(f32[4,256,128]{2,1,0:T(8,128)S(1)} %get-tuple-element.72), channel_id=1, source_target_pairs={{0,2},{2,4},{4,6},{6,7},{7,5},{5,3},{3,1},{1,0},{8,10},{10,12},{12... | collective-permute-start | bytes 1572872 | tf_op jit(solution)/shard_map/ppermute | solution.py:545
  250.9 13.1 %collective-permute-start.14 = (f32[4,256,128]{2,1,0:T(8,128)S(1)}, f32[4,256,128]{2,1,0:T(8,128)S(1)}, u32[]{:S(2)}, u32[]{:S(2)}) collective-permute-start(f32[4,256,128]{2,1,0:T(8,128)S(1)} %get-tuple-element.71), channel_id=1, source_target_pairs={{0,1},{2,0},{4,2},{6,4},{7,6},{5,7},{3,5},{1,3},{8,9},{10,8},{12,1... | collective-permute-start | bytes 1572872 | tf_op jit(solution)/shard_map/ppermute | solution.py:545
  252.6 12.0 %collective-permute-start.7 = (f32[4,256,128]{2,1,0:T(8,128)S(1)}, f32[4,256,128]{2,1,0:T(8,128)S(1)}, u32[]{:S(2)}, u32[]{:S(2)}) collective-permute-start(f32[4,256,128]{2,1,0:T(8,128)S(1)} %get-tuple-element.70), channel_id=1, source_target_pairs={{0,2},{2,4},{4,6},{6,7},{7,5},{5,3},{3,1},{1,0},{8,10},{10,12},{12... | collective-permute-start | bytes 1572872 | tf_op jit(solution)/shard_map/ppermute | solution.py:545
  266.8 12.0 %collective-permute-start.15 = (f32[4,256,128]{2,1,0:T(8,128)}, f32[4,256,128]{2,1,0:T(8,128)}, u32[]{:S(2)}, u32[]{:S(2)}) collective-permute-start(f32[4,256,128]{2,1,0:T(8,128)} %get-tuple-element.69), channel_id=1, source_target_pairs={{0,1},{2,0},{4,2},{6,4},{7,6},{5,7},{3,5},{1,3},{8,9},{10,8},{12,1... | collective-permute-start | bytes 1572872 | tf_op jit(solution)/shard_map/ppermute | solution.py:545
  268.3 11.0 %collective-permute-start.8 = (f32[4,256,128]{2,1,0:T(8,128)S(1)}, f32[4,256,128]{2,1,0:T(8,128)}, u32[]{:S(2)}, u32[]{:S(2)}) collective-permute-start(f32[4,256,128]{2,1,0:T(8,128)S(1)} %get-tuple-element.68), channel_id=1, source_target_pairs={{0,2},{2,4},{4,6},{6,7},{7,5},{5,3},{3,1},{1,0},{8,10},{10,12},{12... | collective-permute-start | bytes 1572872 | tf_op jit(solution)/shard_map/ppermute | solution.py:545
  280.9 17.3 %collective-permute-start.16 = (f32[4,256,128]{2,1,0:T(8,128)S(1)}, f32[4,256,128]{2,1,0:T(8,128)S(1)}, u32[]{:S(2)}, u32[]{:S(2)}) collective-permute-start(f32[4,256,128]{2,1,0:T(8,128)S(1)} %get-tuple-element.67), channel_id=1, source_target_pairs={{0,1},{2,0},{4,2},{6,4},{7,6},{5,7},{3,5},{1,3},{8,9},{10,8},{12,1... | collective-permute-start | bytes 1572872 | tf_op jit(solution)/shard_map/ppermute | solution.py:545
  283.0 15.2 %collective-permute-start.9 = (f32[4,256,128]{2,1,0:T(8,128)S(1)}, f32[4,256,128]{2,1,0:T(8,128)S(1)}, u32[]{:S(2)}, u32[]{:S(2)}) collective-permute-start(f32[4,256,128]{2,1,0:T(8,128)S(1)} %get-tuple-element.66), channel_id=1, source_target_pairs={{0,2},{2,4},{4,6},{6,7},{7,5},{5,3},{3,1},{1,0},{8,10},{10,12},{12... | collective-permute-start | bytes 1572872 | tf_op jit(solution)/shard_map/ppermute | solution.py:545
  300.3 45.6 %collective-permute-start.10 = (f32[4,256,128]{2,1,0:T(8,128)}, f32[4,256,128]{2,1,0:T(8,128)S(1)}, u32[]{:S(2)}, u32[]{:S(2)}) collective-permute-start(f32[4,256,128]{2,1,0:T(8,128)} %get-tuple-element.64), channel_id=1, source_target_pairs={{0,2},{2,4},{4,6},{6,7},{7,5},{5,3},{3,1},{1,0},{8,10},{10,12},{12... | collective-permute-start | bytes 1572872 | tf_op jit(solution)/shard_map/ppermute | solution.py:545
  301.8 44.0 %collective-permute-start.17 = (f32[4,256,128]{2,1,0:T(8,128)S(1)}, f32[4,256,128]{2,1,0:T(8,128)}, u32[]{:S(2)}, u32[]{:S(2)}) collective-permute-start(f32[4,256,128]{2,1,0:T(8,128)S(1)} %get-tuple-element.65), channel_id=1, source_target_pairs={{0,1},{2,0},{4,2},{6,4},{7,6},{5,7},{3,5},{1,3},{8,9},{10,8},{12,1... | collective-permute-start | bytes 1572872 | tf_op jit(solution)/shard_map/ppermute | solution.py:545
  309.4 56.6 %collective-permute-start.3 = (bf16[128,4736]{1,0:T(8,128)(2,1)}, bf16[128,4736]{1,0:T(8,128)(2,1)}, u32[]{:S(2)}, u32[]{:S(2)}) collective-permute-start(bf16[128,4736]{1,0:T(8,128)(2,1)} %get-tuple-element.81), channel_id=1, source_target_pairs={{0,8},{8,0},{16,24},{24,16},{1,9},{9,1},{17,25},{25,17},{2,10},{10... | collective-permute-start | bytes 3637256 | tf_op jit(solution)/shard_map/ppermute | solution.py:525
  309.4 56.6 %collective-permute-start.4 = (bf16[128,4736]{1,0:T(8,128)(2,1)}, bf16[128,4736]{1,0:T(8,128)(2,1)}, u32[]{:S(2)}, u32[]{:S(2)}) collective-permute-start(bf16[128,4736]{1,0:T(8,128)(2,1)} %get-tuple-element.80), channel_id=1, source_target_pairs={{0,16},{8,24},{16,0},{24,8},{1,17},{9,25},{17,1},{25,9},{2,18},{10... | collective-permute-start | bytes 3637256 | tf_op jit(solution)/shard_map/ppermute | solution.py:525
  310.9 55.0 %collective-permute-start.5 = (bf16[128,4736]{1,0:T(8,128)(2,1)S(1)}, bf16[128,4736]{1,0:T(8,128)(2,1)}, u32[]{:S(2)}, u32[]{:S(2)}) collective-permute-start(bf16[128,4736]{1,0:T(8,128)(2,1)S(1)} %get-tuple-element.79), channel_id=1, source_target_pairs={{0,24},{8,16},{16,8},{24,0},{1,25},{9,17},{17,9},{25,1},{2,26},{10... | collective-permute-start | bytes 3637256 | tf_op jit(solution)/shard_map/ppermute | solution.py:525
  348.3 12.3 %collective-permute-start.11 = (f32[4,256,128]{2,1,0:T(8,128)}, f32[4,256,128]{2,1,0:T(8,128)S(1)}, u32[]{:S(2)}, u32[]{:S(2)}) collective-permute-start(f32[4,256,128]{2,1,0:T(8,128)} %get-tuple-element.62), channel_id=1, source_target_pairs={{0,2},{2,4},{4,6},{6,7},{7,5},{5,3},{3,1},{1,0},{8,10},{10,12},{12... | collective-permute-start | bytes 1572872 | tf_op jit(solution)/shard_map/ppermute | solution.py:545
  349.6 11.8 %collective-permute-start.18 = (f32[4,256,128]{2,1,0:T(8,128)}, f32[4,256,128]{2,1,0:T(8,128)}, u32[]{:S(2)}, u32[]{:S(2)}) collective-permute-start(f32[4,256,128]{2,1,0:T(8,128)} %get-tuple-element.63), channel_id=1, source_target_pairs={{0,1},{2,0},{4,2},{6,4},{7,6},{5,7},{3,5},{1,3},{8,9},{10,8},{12,1... | collective-permute-start | bytes 1572872 | tf_op jit(solution)/shard_map/ppermute | solution.py:545
  351.3 20.0 %all-to-all-start.2 = ((f32[4,1,15152]{2,1,0:T(1,128)}), f32[4,1,15152]{2,1,0:T(1,128)S(1)}, u32[]{:S(2)}, u32[]{:S(2)}) async-start(f32[4,1,15152]{2,1,0:T(1,128)} %all_to_all.18), calls=%async_computation.3 | async-start | bytes 487424 | tf_op jit(solution)/shard_map/all_to_all | solution.py:688
  364.8 10.9 %collective-permute-start.19 = (f32[4,256,128]{2,1,0:T(8,128)}, f32[4,256,128]{2,1,0:T(8,128)}, u32[]{:S(2)}, u32[]{:S(2)}) collective-permute-start(f32[4,256,128]{2,1,0:T(8,128)} %get-tuple-element.61), channel_id=1, source_target_pairs={{0,1},{2,0},{4,2},{6,4},{7,6},{5,7},{3,5},{1,3},{8,9},{10,8},{12,1... | collective-permute-start | bytes 1572872 | tf_op jit(solution)/shard_map/ppermute | solution.py:545
  (14 other events, 92.6 us)
Sparse Core Ops, SparseCore 0:
  10.1 87.4 all-gather.1
  275.1 66.7 reduce-scatter.1

commit v4 on v3

--- a/solution.py
+++ b/solution.py
@@ -676,6 +676,7 @@
     payload = jnp.pad(payload, ((0, 0), (0, lines * 128 - used))).reshape(fsdp_count, lines, 128)
     summed = lax.psum_scatter(payload, "fsdp", scatter_dimension=0, tiled=False)
     summed = summed.reshape(-1)[:used]
+    summed = jnp.where(dp_at < 0, grad_states[0, 0, 0, 0], summed)
     tail_size = prompt_count * 3 * chan_share
     shared = summed[dp_count * tail_size :]
     pieces = jnp.concatenate(

time: 387 us -> 411 us (1.062)
  waiting for transfers between devices: 111 us -> 141 us
    ppermute x6, waiting for transfers between devices: 0.02 us -> 14.3 us  [swap_blocks(): lax.ppermute(blocks[o], 'dp', [(i, i ^ o) for i in range(count)])]
    ppermute x14, waiting for transfers between devices: 31.7 us -> 45.6 us  [ring_sums(): held[way] = lax.ppermute(held[way], 'fsdp', pairs) + part(way, hop)]
    all_to_all x2, waiting for transfers between devices: 47.5 us -> 54.6 us  [to_all(): return lax.all_to_all(many, axes, split_axis=0, concat_axis=0, tiled=True)]
    reduce_scatter x1, waiting for transfers between devices: 30.7 us -> 26.2 us  [shards(): summed = lax.psum_scatter(payload, 'fsdp', scatter_dimension=0, tiled=False)]
    unnamed x33 -> x35, local copies, waits for them, and re-layouts: 7.71 us -> 8.68 us
  transfers between devices with their start and end apart: 25 -> 25, of which waited for: 10 -> 15; matrix products, arithmetic and copies ran while one was open for 14% -> 11% of each run, Pallas kernels for 1% -> 1%
where the time goes in v4:
time: 411 us; the launch traced here: 408 us
  waiting for transfers between devices  141 us (34%)
  Pallas kernels  112 us (27%)
  between operations  55.2 us (13%)
  local copies, waits for them, and re-layouts  39 us (9%)
  starting transfers between devices  35.4 us (9%)
  other arithmetic  23.9 us (6%)
    pallas_call x1, Pallas kernels, run_mixer(): pl.pallas_call(functools.partial(mixer_kernel, dims), grid=(blocks,), in_...  108 us
    all_to_all x2, waiting for transfers between devices, to_all(): return lax.all_to_all(many, axes, split_axis=0, concat_axis=0, tiled=True)  54.6 us
    ppermute x14, waiting for transfers between devices, ring_sums(): held[way] = lax.ppermute(held[way], 'fsdp', pairs) + part(way, hop)  45.6 us
    reduce_scatter x1, waiting for transfers between devices, shards(): summed = lax.psum_scatter(payload, 'fsdp', scatter_dimension=0, tiled=False)  26.2 us
    ppermute x14, starting transfers between devices, ring_sums(): held[way] = lax.ppermute(held[way], 'fsdp', pairs) + part(way, hop)  14.6 us
    ppermute x6, waiting for transfers between devices, swap_blocks(): lax.ppermute(blocks[o], 'dp', [(i, i ^ o) for i in range(count)])  14.3 us
    all_to_all x2, starting transfers between devices, to_all(): return lax.all_to_all(many, axes, split_axis=0, concat_axis=0, tiled=True)  13.3 us
    add x7, other arithmetic, ring_sums(): held[way] = lax.ppermute(held[way], 'fsdp', pairs) + part(way, hop)  11.3 us
  transfers between devices with their start and end apart: 25, of which 15 were waited for; matrix products, arithmetic and copies ran while one was open for 11% of the time, Pallas kernels for 1%

profile of v4, /device:TPU:0, one launch (start us, length us, event | category | flops | bytes accessed | tf_op | source)
XLA Modules:
  0.0 408.2 jit_solution(2125537610921590633)
XLA Ops:
  10.3 7.3 %all-to-all-start.1 = ((f32[8,1,7472]{2,1,0:T(1,128)}), f32[8,1,7472]{2,1,0:T(1,128)S(1)}, u32[]{:S(2)}, u32[]{:S(2)}) async-start(f32[8,1,7472]{2,1,0:T(1,128)} %broadcast_in_dim.27), calls=%async_computation.1 | async-start | bytes 483328 | tf_op jit(solution)/shard_map/all_to_all | solution.py:551
  21.0 1.8 copy-done.2
  26.0 2.5 fusion.20
  51.0 6.0 %all-to-all-start = ((bf16[32,8,3,320]{3,1,2,0:T(8,128)(2,1)}), bf16[32,8,3,320]{3,1,2,0:T(8,128)(2,1)S(1)}, u32[]{:S(2)}, u32[]{:S(2)}) async-start(bf16[32,8,3,320]{3,1,2,0:T(8,128)(2,1)} %broadcast_in_dim.26), calls=%async_computation | async-start | bytes 1179648 | tf_op jit(solution)/shard_map/all_to_all | solution.py:551
  59.0 54.6 %all-to-all-done = bf16[32,8,3,320]{3,1,2,0:T(8,128)(2,1)S(1)} async-done(((bf16[32,8,3,320]{3,1,2,0:T(8,128)(2,1)}), bf16[32,8,3,320]{3,1,2,0:T(8,128)(2,1)S(1)}, u32[]{:S(2)}, u32[]{:S(2)}) %all-to-all-start) | async-done | bytes 491552 | tf_op jit(solution)/shard_map/all_to_all | solution.py:551
  118.9 6.0 %pad_maximum_fusion.recv_ref = bf16[4,128,6784]{2,1,0:T(8,128)(2,1)} fusion(bf16[1,128,6784]{2,1,0:T(8,128)(2,1)} %bitcast.15, bf16[1,128,6784]{2,1,0:T(8,128)(2,1)} %bitcast.13, bf16[1,128,6784]{2,1,0:T(8,128)(2,1)} %bitcast.11, bf16[1,128,6784]{2,1,0:T(8,128)(2,1)S(1)} %get-tuple-element.74), kind=kLoop, calls=%fused_computation.3 | loop fusion | flops 10420224 | bytes 13893632 | tf_op jit(solution)/shard_map/stack | solution.py:526
  124.9 107.5 %mixer.1 = (bf16[4,128,4736]{2,1,0:T(8,128)(2,1)}, f32[8,8,256,128]{3,2,1,0:T(8,128)}, f32[4,16,2560]{2,1,0:T(8,128)}, f32[16,2560]{1,0:T(8,128)}) custom-call(s32[16]{0:T(128)} %reshape.210.prompt_ref, f32[16]{0:T(128)} %reshape.212.adv_ref, bf16[4,128,6784]{2,1,0:T(8,128)(2,1)} %pad_maximum_fusion.recv_ref, bf16[4,16,2560]{2,1,0:T(8,128)(2,1)} %reshape.215.tails_ref, ...), custom_call_target="tpu_custom_call" | custom-call | flops 20000000000 | bytes 30000000 | tf_op jit(solution)/shard_map/mixer/pallas_call | solution.py:379
  239.6 8.1 %collective-permute-done.13 = f32[4,256,128]{2,1,0:T(8,128)S(1)} collective-permute-done((f32[4,256,128]{2,1,0:T(8,128)S(1)}, f32[4,256,128]{2,1,0:T(8,128)S(1)}, u32[]{:S(2)}, u32[]{:S(2)}) %collective-permute-start.13) | collective-permute-done | bytes 524320 | tf_op jit(solution)/shard_map/ppermute | solution.py:545
  266.2 2.3 bitcast_add_fusion.12
  271.0 10.2 %collective-permute-done.15 = f32[4,256,128]{2,1,0:T(8,128)S(1)} collective-permute-done((f32[4,256,128]{2,1,0:T(8,128)}, f32[4,256,128]{2,1,0:T(8,128)S(1)}, u32[]{:S(2)}, u32[]{:S(2)}) %collective-permute-start.15) | collective-permute-done | bytes 524320 | tf_op jit(solution)/shard_map/ppermute | solution.py:545
  285.1 9.0 %collective-permute-done.16 = f32[4,256,128]{2,1,0:T(8,128)S(1)} collective-permute-done((f32[4,256,128]{2,1,0:T(8,128)S(1)}, f32[4,256,128]{2,1,0:T(8,128)S(1)}, u32[]{:S(2)}, u32[]{:S(2)}) %collective-permute-start.16) | collective-permute-done | bytes 524320 | tf_op jit(solution)/shard_map/ppermute | solution.py:545
  294.9 2.3 bitcast_add_fusion.10
  305.4 2.4 collective-permute-done.10
  319.2 6.6 %collective-permute-done.11 = f32[4,256,128]{2,1,0:T(8,128)S(1)} collective-permute-done((f32[4,256,128]{2,1,0:T(8,128)S(1)}, f32[4,256,128]{2,1,0:T(8,128)S(1)}, u32[]{:S(2)}, u32[]{:S(2)}) %collective-permute-start.11) | collective-permute-done | bytes 524320 | tf_op jit(solution)/shard_map/ppermute | solution.py:545
  325.7 3.8 collective-permute-done.18
  330.8 2.2 collective-permute-start.12
  333.1 4.2 %fusion.21 = (bf16[1,128,4736]{2,1,0:T(8,128)(2,1)S(1)}, bf16[128,4736]{1,0:T(8,128)(2,1)S(1)}, bf16[128,4736]{1,0:T(8,128)(2,1)}, bf16[128,4736]{1,0:T(8,128)(2,1)}) fusion(bf16[4,128,4736]{2,1,0:T(8,128)(2,1)} %get-tuple-element.18), kind=kLoop, calls=%fused_computation.87 | loop fusion | bytes 9699328 | tf_op jit(solution)/shard_map/slice | solution.py:523
  337.2 2.0 collective-permute-start.4
  339.4 2.1 collective-permute-done.12
  346.1 26.2 %reduce-scatter.2.cloned.1.call-done = f32[1,304,128]{2,1,0:T(8,128)} async-done(((f32[8,304,128]{2,1,0:T(8,128)}), f32[1,304,128]{2,1,0:T(8,128)}) %reduce-scatter.2.cloned.1.call-update) | async-done | bytes 155664 | tf_op jit(solution)/shard_map/reduce_scatter | solution.py:677
  375.0 3.4 all-to-all-start.2
  378.4 14.2 %collective-permute-done.5 = bf16[128,4736]{1,0:T(8,128)(2,1)} collective-permute-done((bf16[128,4736]{1,0:T(8,128)(2,1)S(1)}, bf16[128,4736]{1,0:T(8,128)(2,1)}, u32[]{:S(2)}, u32[]{:S(2)}) %collective-permute-start.5) | collective-permute-done | bytes 1212448 | tf_op jit(solution)/shard_map/ppermute | solution.py:525
  392.6 2.4 pad_maximum_fusion.1.back
  395.0 3.0 unpack.1
  (173 shorter events, 62.9 us)
Async XLA Ops:
  7.2 117.7 %all-gather.2.cloned.1.call-start = ((), (), s32[]{:S(2)}) async-start(), calls=%async_computation.4 | async-start | bytes 4718592 | tf_op jit(solution)/shard_map/all_gather | solution.py:588
  10.3 39.8 %all-to-all-start.1 = ((f32[8,1,7472]{2,1,0:T(1,128)}), f32[8,1,7472]{2,1,0:T(1,128)S(1)}, u32[]{:S(2)}, u32[]{:S(2)}) async-start(f32[8,1,7472]{2,1,0:T(1,128)} %broadcast_in_dim.27), calls=%async_computation.1 | async-start | bytes 483328 | tf_op jit(solution)/shard_map/all_to_all | solution.py:551
  28.5 90.4 %collective-permute-start = (bf16[128,6784]{1,0:T(8,128)(2,1)}, bf16[128,6784]{1,0:T(8,128)(2,1)}, u32[]{:S(2)}, u32[]{:S(2)}) collective-permute-start(bf16[128,6784]{1,0:T(8,128)(2,1)} %get-tuple-element.77), channel_id=1, source_target_pairs={{0,8},{8,0},{16,24},{24,16},{1,9},{9,1},{17,25},{25,17},{2,10},{10... | collective-permute-start | bytes 5210120 | tf_op jit(solution)/shard_map/ppermute | solution.py:525
  28.5 90.4 %collective-permute-start.1 = (bf16[128,6784]{1,0:T(8,128)(2,1)}, bf16[128,6784]{1,0:T(8,128)(2,1)}, u32[]{:S(2)}, u32[]{:S(2)}) collective-permute-start(bf16[128,6784]{1,0:T(8,128)(2,1)} %get-tuple-element.76), channel_id=1, source_target_pairs={{0,16},{8,24},{16,0},{24,8},{1,17},{9,25},{17,1},{25,9},{2,18},{10... | collective-permute-start | bytes 5210120 | tf_op jit(solution)/shard_map/ppermute | solution.py:525
  29.9 89.0 %collective-permute-start.2 = (bf16[128,6784]{1,0:T(8,128)(2,1)}, bf16[128,6784]{1,0:T(8,128)(2,1)}, u32[]{:S(2)}, u32[]{:S(2)}) collective-permute-start(bf16[128,6784]{1,0:T(8,128)(2,1)} %get-tuple-element.75), channel_id=1, source_target_pairs={{0,24},{8,16},{16,8},{24,0},{1,25},{9,17},{17,9},{25,1},{2,26},{10... | collective-permute-start | bytes 5210120 | tf_op jit(solution)/shard_map/ppermute | solution.py:525
  51.0 62.6 %all-to-all-start = ((bf16[32,8,3,320]{3,1,2,0:T(8,128)(2,1)}), bf16[32,8,3,320]{3,1,2,0:T(8,128)(2,1)S(1)}, u32[]{:S(2)}, u32[]{:S(2)}) async-start(bf16[32,8,3,320]{3,1,2,0:T(8,128)(2,1)} %broadcast_in_dim.26), calls=%async_computation | async-start | bytes 1179648 | tf_op jit(solution)/shard_map/all_to_all | solution.py:551
  57.0 315.4 %reduce-scatter.2.cloned.1.call-start = ((), (), s32[]{:S(2)}) async-start(), calls=%async_computation.5 | async-start | bytes 1400832 | tf_op jit(solution)/shard_map/reduce_scatter | solution.py:677
  233.7 14.0 %collective-permute-start.13 = (f32[4,256,128]{2,1,0:T(8,128)S(1)}, f32[4,256,128]{2,1,0:T(8,128)S(1)}, u32[]{:S(2)}, u32[]{:S(2)}) collective-permute-start(f32[4,256,128]{2,1,0:T(8,128)S(1)} %get-tuple-element.73), channel_id=1, source_target_pairs={{0,1},{2,0},{4,2},{6,4},{7,6},{5,7},{3,5},{1,3},{8,9},{10,8},{12,1... | collective-permute-start | bytes 1572872 | tf_op jit(solution)/shard_map/ppermute | solution.py:545
  234.7 13.0 %collective-permute-start.6 = (f32[4,256,128]{2,1,0:T(8,128)S(1)}, f32[4,256,128]{2,1,0:T(8,128)S(1)}, u32[]{:S(2)}, u32[]{:S(2)}) collective-permute-start(f32[4,256,128]{2,1,0:T(8,128)S(1)} %get-tuple-element.72), channel_id=1, source_target_pairs={{0,2},{2,4},{4,6},{6,7},{7,5},{5,3},{3,1},{1,0},{8,10},{10,12},{12... | collective-permute-start | bytes 1572872 | tf_op jit(solution)/shard_map/ppermute | solution.py:545
  249.1 17.1 %collective-permute-start.14 = (f32[4,256,128]{2,1,0:T(8,128)S(1)}, f32[4,256,128]{2,1,0:T(8,128)S(1)}, u32[]{:S(2)}, u32[]{:S(2)}) collective-permute-start(f32[4,256,128]{2,1,0:T(8,128)S(1)} %get-tuple-element.71), channel_id=1, source_target_pairs={{0,1},{2,0},{4,2},{6,4},{7,6},{5,7},{3,5},{1,3},{8,9},{10,8},{12,1... | collective-permute-start | bytes 1572872 | tf_op jit(solution)/shard_map/ppermute | solution.py:545
  250.8 15.4 %collective-permute-start.7 = (f32[4,256,128]{2,1,0:T(8,128)S(1)}, f32[4,256,128]{2,1,0:T(8,128)}, u32[]{:S(2)}, u32[]{:S(2)}) collective-permute-start(f32[4,256,128]{2,1,0:T(8,128)S(1)} %get-tuple-element.70), channel_id=1, source_target_pairs={{0,2},{2,4},{4,6},{6,7},{7,5},{5,3},{3,1},{1,0},{8,10},{10,12},{12... | collective-permute-start | bytes 1572872 | tf_op jit(solution)/shard_map/ppermute | solution.py:545
  268.5 12.7 %collective-permute-start.15 = (f32[4,256,128]{2,1,0:T(8,128)}, f32[4,256,128]{2,1,0:T(8,128)S(1)}, u32[]{:S(2)}, u32[]{:S(2)}) collective-permute-start(f32[4,256,128]{2,1,0:T(8,128)} %get-tuple-element.69), channel_id=1, source_target_pairs={{0,1},{2,0},{4,2},{6,4},{7,6},{5,7},{3,5},{1,3},{8,9},{10,8},{12,1... | collective-permute-start | bytes 1572872 | tf_op jit(solution)/shard_map/ppermute | solution.py:545
  270.2 11.5 %collective-permute-start.8 = (f32[4,256,128]{2,1,0:T(8,128)S(1)}, f32[4,256,128]{2,1,0:T(8,128)S(1)}, u32[]{:S(2)}, u32[]{:S(2)}) collective-permute-start(f32[4,256,128]{2,1,0:T(8,128)S(1)} %get-tuple-element.68), channel_id=1, source_target_pairs={{0,2},{2,4},{4,6},{6,7},{7,5},{5,3},{3,1},{1,0},{8,10},{10,12},{12... | collective-permute-start | bytes 1572872 | tf_op jit(solution)/shard_map/ppermute | solution.py:545
  283.0 11.1 %collective-permute-start.16 = (f32[4,256,128]{2,1,0:T(8,128)S(1)}, f32[4,256,128]{2,1,0:T(8,128)S(1)}, u32[]{:S(2)}, u32[]{:S(2)}) collective-permute-start(f32[4,256,128]{2,1,0:T(8,128)S(1)} %get-tuple-element.67), channel_id=1, source_target_pairs={{0,1},{2,0},{4,2},{6,4},{7,6},{5,7},{3,5},{1,3},{8,9},{10,8},{12,1... | collective-permute-start | bytes 1572872 | tf_op jit(solution)/shard_map/ppermute | solution.py:545
  284.5 10.4 %collective-permute-start.9 = (f32[4,256,128]{2,1,0:T(8,128)S(1)}, f32[4,256,128]{2,1,0:T(8,128)S(1)}, u32[]{:S(2)}, u32[]{:S(2)}) collective-permute-start(f32[4,256,128]{2,1,0:T(8,128)S(1)} %get-tuple-element.66), channel_id=1, source_target_pairs={{0,2},{2,4},{4,6},{6,7},{7,5},{5,3},{3,1},{1,0},{8,10},{10,12},{12... | collective-permute-start | bytes 1572872 | tf_op jit(solution)/shard_map/ppermute | solution.py:545
  297.2 10.7 %collective-permute-start.10 = (f32[4,256,128]{2,1,0:T(8,128)}, f32[4,256,128]{2,1,0:T(8,128)S(1)}, u32[]{:S(2)}, u32[]{:S(2)}) collective-permute-start(f32[4,256,128]{2,1,0:T(8,128)} %get-tuple-element.64), channel_id=1, source_target_pairs={{0,2},{2,4},{4,6},{6,7},{7,5},{5,3},{3,1},{1,0},{8,10},{10,12},{12... | collective-permute-start | bytes 1572872 | tf_op jit(solution)/shard_map/ppermute | solution.py:545
  309.6 16.1 %collective-permute-start.11 = (f32[4,256,128]{2,1,0:T(8,128)S(1)}, f32[4,256,128]{2,1,0:T(8,128)S(1)}, u32[]{:S(2)}, u32[]{:S(2)}) collective-permute-start(f32[4,256,128]{2,1,0:T(8,128)S(1)} %get-tuple-element.62), channel_id=1, source_target_pairs={{0,2},{2,4},{4,6},{6,7},{7,5},{5,3},{3,1},{1,0},{8,10},{10,12},{12... | collective-permute-start | bytes 1572872 | tf_op jit(solution)/shard_map/ppermute | solution.py:545
  311.1 18.4 %collective-permute-start.18 = (f32[4,256,128]{2,1,0:T(8,128)S(1)}, f32[4,256,128]{2,1,0:T(8,128)S(1)}, u32[]{:S(2)}, u32[]{:S(2)}) collective-permute-start(f32[4,256,128]{2,1,0:T(8,128)S(1)} %get-tuple-element.63), channel_id=1, source_target_pairs={{0,1},{2,0},{4,2},{6,4},{7,6},{5,7},{3,5},{1,3},{8,9},{10,8},{12,1... | collective-permute-start | bytes 1572872 | tf_op jit(solution)/shard_map/ppermute | solution.py:545
  330.8 10.7 %collective-permute-start.12 = (f32[4,256,128]{2,1,0:T(8,128)S(1)}, f32[4,256,128]{2,1,0:T(8,128)S(1)}, u32[]{:S(2)}, u32[]{:S(2)}) collective-permute-start(f32[4,256,128]{2,1,0:T(8,128)S(1)} %get-tuple-element.60), channel_id=1, source_target_pairs={{0,2},{2,4},{4,6},{6,7},{7,5},{5,3},{3,1},{1,0},{8,10},{10,12},{12... | collective-permute-start | bytes 1572872 | tf_op jit(solution)/shard_map/ppermute | solution.py:545
  333.1 10.2 %collective-permute-start.19 = (f32[4,256,128]{2,1,0:T(8,128)S(1)}, f32[4,256,128]{2,1,0:T(8,128)S(1)}, u32[]{:S(2)}, u32[]{:S(2)}) collective-permute-start(f32[4,256,128]{2,1,0:T(8,128)S(1)} %get-tuple-element.61), channel_id=1, source_target_pairs={{0,1},{2,0},{4,2},{6,4},{7,6},{5,7},{3,5},{1,3},{8,9},{10,8},{12,1... | collective-permute-start | bytes 1572872 | tf_op jit(solution)/shard_map/ppermute | solution.py:545
  337.2 41.1 %collective-permute-start.3 = (bf16[128,4736]{1,0:T(8,128)(2,1)}, bf16[128,4736]{1,0:T(8,128)(2,1)}, u32[]{:S(2)}, u32[]{:S(2)}) collective-permute-start(bf16[128,4736]{1,0:T(8,128)(2,1)} %get-tuple-element.81), channel_id=1, source_target_pairs={{0,8},{8,0},{16,24},{24,16},{1,9},{9,1},{17,25},{25,17},{2,10},{10... | collective-permute-start | bytes 3637256 | tf_op jit(solution)/shard_map/ppermute | solution.py:525
  337.2 41.2 %collective-permute-start.4 = (bf16[128,4736]{1,0:T(8,128)(2,1)}, bf16[128,4736]{1,0:T(8,128)(2,1)}, u32[]{:S(2)}, u32[]{:S(2)}) collective-permute-start(bf16[128,4736]{1,0:T(8,128)(2,1)} %get-tuple-element.80), channel_id=1, source_target_pairs={{0,16},{8,24},{16,0},{24,8},{1,17},{9,25},{17,1},{25,9},{2,18},{10... | collective-permute-start | bytes 3637256 | tf_op jit(solution)/shard_map/ppermute | solution.py:525
  339.2 53.4 %collective-permute-start.5 = (bf16[128,4736]{1,0:T(8,128)(2,1)S(1)}, bf16[128,4736]{1,0:T(8,128)(2,1)}, u32[]{:S(2)}, u32[]{:S(2)}) collective-permute-start(bf16[128,4736]{1,0:T(8,128)(2,1)S(1)} %get-tuple-element.79), channel_id=1, source_target_pairs={{0,24},{8,16},{16,8},{24,0},{1,25},{9,17},{17,9},{25,1},{2,26},{10... | collective-permute-start | bytes 3637256 | tf_op jit(solution)/shard_map/ppermute | solution.py:525
  375.0 23.0 %all-to-all-start.2 = ((f32[4,1,15152]{2,1,0:T(1,128)}), f32[4,1,15152]{2,1,0:T(1,128)S(1)}, u32[]{:S(2)}, u32[]{:S(2)}) async-start(f32[4,1,15152]{2,1,0:T(1,128)} %all_to_all.18), calls=%async_computation.3 | async-start | bytes 487424 | tf_op jit(solution)/shard_map/all_to_all | solution.py:689
  (15 other events, 128.8 us)
Sparse Core Ops, SparseCore 0:
  10.1 87.4 all-gather.1
  305.5 66.7 reduce-scatter.1
